TPU v7x, 512 devices: a whole 4x8x8 slice. The times are simulated.
512 devices in a mesh: cols: 4 (over y_lo), dom: 128 (over z, y_hi, x, core).
Axes of the slice: x: 4, y: 8 (y_hi: 2, y_lo: 4; y = y_hi * 4 + y_lo), z: 8, core: 2. Of those that a mesh axis runs over, the one named last changes fastest.
Arguments:
- features: bfloat16 [768, 65536], P('cols', 'dom'), may hold values from -6 to 6
- proj_in: bfloat16 [768, 256], P('cols'), may hold values from -0.3125 to 0.3125
- self_weight: bfloat16 [256, 256], replicated, may hold values from -0.375 to 0.375
- neigh_weight: bfloat16 [256, 256], replicated, may hold values from -0.375 to 0.375
- neighbors: int32 [16, 65536], P(None, 'dom'), may hold values from 0 to 8703, as said below
- degree: int32 [65536], P('dom'), may hold values from 1 to 16
- send_rows: int32 [128, 8192], P('dom'), may hold values from 0 to 511
- send_count: int32 [128, 128], P('dom'), may hold values from 0 to 64, as said below
Outputs:
- layer_out: bfloat16 [256, 65536], P('cols', 'dom')
Inputs may be any that keep to these rules, and one draw needn't show every extreme that they name: `neighbors`: A code at or above 512 names a source partition other than the node's own and a slot below send_count of that source towards the node's partition. Every partition's rows are received in full (64 slots) from every other partition for at least one partition in every draw. `send_count`: zero on the diagonal; elsewhere 1 to 64, and 64 from every source towards at least one partition.
All inputs are finite; a program needn't handle non-finite values.
Results may differ from a plain program's by a relative error of at most 0.0051.
Values may be sent and summed in bfloat16 or wider, within the bound.
No kernel may reach another device: no remote copies, remote signals or barrier semaphores. Data moves between devices by JAX's collectives and lax.ppermute only.
A program may use at most 64 MiB of HBM per device.

v0:
```python
import math

import jax
import jax.numpy as jnp
from jax import lax
from jax.sharding import PartitionSpec as P


def cut_along(shard, dim, size):
    before, after = (shard.shape[:dim], shard.shape[dim + 1 :])
    return jnp.moveaxis(shard.reshape(*before, size, -1, *after), dim, 0)


def sent_and_summed(shard, axis, dim):
    size = lax.axis_size(axis)
    blocks = lax.all_to_all(cut_along(shard, dim, size), axis, 0, 0, tiled=True)
    return jnp.sum(blocks, axis=0)


def lead_dot(left, right):
    return lax.dot_general(
        left, right, (((0,), (0,)), ((), ())), preferred_element_type=jnp.float32
    )


def local(features, proj_in, self_weight, neigh_weight, neighbors, degree, send_rows, send_count):
    partial_value = lead_dot(proj_in, features)
    hidden = sent_and_summed(partial_value, "cols", 0).astype(jnp.bfloat16)
    width = hidden.shape[0]
    nodes_here = hidden.shape[1]
    parts = lax.axis_size("dom")
    slots = send_rows.shape[1]
    capacity = slots // parts
    lane = jnp.arange(slots, dtype=jnp.int32)
    live = lane % capacity < send_count[0][lane // capacity]
    send_block = math.gcd(slots, 1024)
    send_groups = slots // send_block
    node_iota = jnp.arange(nodes_here, dtype=jnp.int32)[:, None]

    def select_rows(inputs):
        wanted, alive = inputs
        onehot = jnp.logical_and(node_iota == wanted[None, :], alive[None, :]).astype(jnp.bfloat16)
        return jnp.dot(hidden, onehot, preferred_element_type=jnp.float32).astype(jnp.bfloat16)

    chosen = lax.map(
        select_rows,
        (send_rows[0].reshape(send_groups, send_block), live.reshape(send_groups, send_block)),
    )
    outgoing = jnp.transpose(chosen, (1, 0, 2)).reshape(width, slots)
    incoming = lax.all_to_all(outgoing, "dom", split_axis=1, concat_axis=1, tiled=True)
    table = jnp.concatenate([hidden, incoming], axis=1)
    table_rows = table.shape[1]
    slot_count = neighbors.shape[0]
    used = jnp.arange(slot_count, dtype=jnp.int32)[:, None] < degree[None, :]
    codes = jnp.where(used, neighbors, -1)
    node_block = math.gcd(nodes_here, 256)
    node_groups = nodes_here // node_block
    grouped = jnp.transpose(codes.reshape(slot_count, node_groups, node_block), (1, 0, 2))
    table_iota = jnp.arange(table_rows, dtype=jnp.int32)[:, None]

    def aggregate(block_codes):
        counts = jnp.zeros((table_rows, node_block), jnp.bfloat16)
        for slot in range(slot_count):
            counts = counts + (table_iota == block_codes[slot][None, :]).astype(jnp.bfloat16)
        return jnp.dot(table, counts, preferred_element_type=jnp.float32)

    summed = lax.map(aggregate, grouped)
    total = jnp.transpose(summed, (1, 0, 2)).reshape(width, nodes_here)
    mean = (total / degree[None, :].astype(jnp.float32)).astype(jnp.bfloat16)
    column = lax.axis_index("cols")
    self_cols = lax.dynamic_slice_in_dim(self_weight, column * width, width, 1)
    neigh_cols = lax.dynamic_slice_in_dim(neigh_weight, column * width, width, 1)
    carry = lead_dot(self_cols, lax.all_gather(hidden, "cols", axis=0, tiled=True))
    result = carry + lead_dot(neigh_cols, lax.all_gather(mean, "cols", axis=0, tiled=True))
    return jnp.maximum(result, 0.0).astype(jnp.bfloat16)


def solution(mesh):
    return jax.shard_map(
        local,
        mesh=mesh,
        in_specs=(
            P("cols", "dom"),
            P("cols", None),
            P(),
            P(),
            P(None, "dom"),
            P("dom"),
            P("dom", None),
            P("dom", None),
        ),
        out_specs=P("cols", "dom"),
        check_vma=False,
    )
```

profile of v0, /device:TPU:2, one launch (start us, length us, event | category | flops | bytes accessed | tf_op | source)
XLA Modules:
  0.0 177.2 jit_solution(613362383656732762)
XLA Ops:
  0.0 0.0 copy-start
  0.0 0.0 copy-start.1
  0.0 0.9 copy-done
  0.9 1.9 %fusion.98 = f32[256,512]{1,0:T(8,128)} fusion(bf16[192,256]{1,0:T(8,128)(2,1)} %param.13, bf16[192,512]{1,0:T(8,128)(2,1)S(1)} %copy-done), kind=kOutput, calls=%fused_computation.119 | convolution fusion | flops 50331648 | bytes 819200 | tf_op jit(solution)/shard_map/dot_general | solution.py:21
  2.9 4.9 %all-to-all-start = ((f32[4,64,512]{2,1,0:T(8,128)}), f32[4,64,512]{2,1,0:T(8,128)S(1)}, u32[]{:S(2)}, u32[]{:S(2)}) async-start(f32[4,64,512]{2,1,0:T(8,128)} %bitcast), calls=%async_computation | async-start | bytes 1048576 | tf_op jit(solution)/shard_map/all_to_all | solution.py:16
  7.8 0.0 copy-done.1
  7.8 0.0 copy-start.5
  7.8 48.9 %gather_fusion = s32[8192]{0:T(1024)S(1)} fusion(s32[128]{0:T(128)S(1)} %bitcast.121, s32[8192]{0:T(1024)S(1)} %broadcast_clamp_fusion), kind=kCustom, calls=%fused_computation | custom fusion | bytes 98304 | tf_op jit(solution)/shard_map/gather | solution.py:35
  56.7 0.5 broadcast.82
  57.2 0.0 copy-done.5
  57.2 0.7 reduce.5
  58.0 0.0 all-to-all-done
  58.0 4.8 %while.23 = (s32[]{:T(128)}, bf16[8,64,1024]{2,1,0:T(8,128)(2,1)S(1)}, s32[8,1024]{1,0:T(8,128)S(1)}, pred[8,1024]{1,0:T(8,128)(4,1)S(1)}, bf16[64,512]{1,0:T(8,128)(2,1)S(1)}, /*index=5*/s32[]{:T(128)}) while((s32[]{:T(128)}, bf16[8,64,1024]{2,1,0:T(8,128)(2,1)S(1)}, s32[8,1024]{1,0:T(8,128)S(1)}, pred[8,1024]{1,0:T(8,128)(4,1)S(1)}, ...), condition=%wide.region_2.3_spmd.clone, body=%wide.region_1.2_spmd.clone.sunk | while | flops 68222976 | bytes 212049 | solution.py:45
  58.1 0.5 fusion.113
  58.7 0.5 fusion.113
  59.3 0.5 fusion.113
  59.9 0.5 fusion.113
  60.5 0.5 fusion.113
  61.1 0.5 fusion.113
  61.7 0.5 fusion.113
  62.3 0.5 fusion.113
  62.8 0.6 copy.12
  63.4 1.3 all_to_all.12
  64.8 2.7 %copy.36 = bf16[64,128,64]{2,0,1:T(8,128)(2,1)} copy(bf16[64,128,64]{2,1,0:T(8,128)(2,1)S(1)} %all_to_all.12) | data formatting | bytes 2097152 | tf_op jit(solution)/shard_map/all_to_all | solution.py:50
  67.5 0.0 copy-start.8
  67.5 0.0 copy-start.6
  67.5 0.0 copy-start.7
  67.5 4.7 %reshape.115 = bf16[128,2,2048]{2,1,0:T(2,128)(2,1)} reshape(bf16[128,64,64]{2,1,0:T(8,128)(2,1)} %bitcast.122) | data formatting | bytes 2097152
  72.2 18.5 %all-to-all-start.1 = ((bf16[128,2,2048]{2,1,0:T(2,128)(2,1)}), bf16[128,2,2048]{2,1,0:T(2,128)(2,1)S(1)}, u32[]{:S(2)}, u32[]{:S(2)}) async-start(bf16[128,2,2048]{2,1,0:T(2,128)(2,1)} %reshape.115), calls=%async_computation.1 | async-start | bytes 2097152 | tf_op jit(solution)/shard_map/all_to_all | solution.py:50
  90.8 0.0 copy-done.8
  90.8 0.0 copy-done.6
  90.8 0.6 reshape.95
  91.4 34.1 %all_gather.6 = bf16[256,512]{1,0:T(8,128)(2,1)S(1)} all-gather(bf16[64,512]{1,0:T(8,128)(2,1)S(1)} %get-tuple-element.374), channel_id=1, replica_groups=mesh['cols'=4,'dom'=128] {'cols'}, dimensions={0}, use_global_device_ids=true | all-gather | bytes 327680 | tf_op jit(solution)/shard_map/all_gather | solution.py:73
  125.5 0.0 copy-done.7
  125.5 0.3 fusion.91
  125.8 0.0 all-to-all-done.1
  125.8 1.4 reshape.116
  127.2 2.7 %copy.14 = bf16[64,128,64]{2,1,0:T(8,128)(2,1)} copy(bf16[64,128,64]{2,0,1:T(8,128)(2,1)S(1)} %bitcast.123) | data formatting | bytes 2097152 | tf_op jit(solution)/shard_map/all_to_all | solution.py:50
  129.9 0.0 copy-start.2
  129.9 0.0 copy-start.3
  129.9 3.3 %all_to_all.14 = bf16[64,8192]{1,0:T(8,128)(2,1)S(1)} reshape(bf16[64,128,64]{2,1,0:T(8,128)(2,1)} %copy.14) | data formatting | bytes 2097152 | tf_op jit(solution)/shard_map/all_to_all | solution.py:50
  133.3 0.1 pad_maximum_fusion
  133.3 0.0 copy-done.2
  133.3 0.0 copy-done.3
  133.4 0.0 copy-start.4
  133.4 28.4 %while.24 = (s32[]{:T(128)}, f32[2,64,256]{2,1,0:T(8,128)S(1)}, s32[2,16,256]{2,0,1:T(2,128)S(1)}, bf16[64,8704]{1,0:T(8,128)(2,1)S(1)}, s32[]{:T(128)}, /*index...) while((s32[]{:T(128)}, f32[2,64,256]{2,1,0:T(8,128)S(1)}, ...), condition=%wide.region_4.5_spmd.clone.clone, body=%wide.region_3.4_spmd.clone.clone.sunk | while | flops 427819008 | bytes 1229237 | solution.py:67
  133.6 0.1 constant_dynamic-slice_fusion.20
  133.6 14.0 %fusion.116 = f32[2,64,256]{2,1,0:T(8,128)S(1)} fusion(f32[2,64,256]{2,1,0:T(8,128)S(1)} %get-tuple-element.331, s32[]{:T(128)} %get-tuple-element.330, bf16[64,8704]{1,0:T(8,128)(2,1)S(1)} %get-tuple-element.354, s32[256]{0:T(256)S(1)} %bitcast.145, s32[256]{0:T(256)S(1)} %bitcast.131, s32[256]{0:T(256)S(1)} %bitcast.132, s32[256]{0:T(256)S(1)} %bitcast.133, ...), kind=kOutput, calls=%fused_computation.68.clone.1 | convolution fusion | flops 427819008 | bytes 1196036 | tf_op jit(solution)/shard_map/while/body/eval_jaxpr/dot_general | solution.py:65
  147.7 0.1 constant_dynamic-slice_fusion.20
  147.8 14.0 %fusion.116 = f32[2,64,256]{2,1,0:T(8,128)S(1)} fusion(f32[2,64,256]{2,1,0:T(8,128)S(1)} %get-tuple-element.331, s32[]{:T(128)} %get-tuple-element.330, bf16[64,8704]{1,0:T(8,128)(2,1)S(1)} %get-tuple-element.354, s32[256]{0:T(256)S(1)} %bitcast.145, s32[256]{0:T(256)S(1)} %bitcast.131, s32[256]{0:T(256)S(1)} %bitcast.132, s32[256]{0:T(256)S(1)} %bitcast.133, ...), kind=kOutput, calls=%fused_computation.68.clone.1 | convolution fusion | flops 427819008 | bytes 1196036 | tf_op jit(solution)/shard_map/while/body/eval_jaxpr/dot_general | solution.py:65
  161.8 14.5 %all_gather.7 = bf16[256,512]{1,0:T(8,128)(2,1)S(1)} all-gather(bf16[64,512]{1,0:T(8,128)(2,1)S(1)} %divide_convert_fusion), channel_id=1, replica_groups=mesh['cols'=4,'dom'=128] {'cols'}, dimensions={0}, use_global_device_ids=true | all-gather | bytes 327680 | tf_op jit(solution)/shard_map/all_gather | solution.py:74
  176.3 0.0 copy-done.4
  176.3 0.9 fusion.89
  (28 shorter events, 0.5 us)
Async XLA Ops:
  0.0 0.9 copy-start
  0.0 7.8 %copy-start.1 = (s32[1,128]{1,0:T(1,128)S(1)}, s32[1,128]{1,0:T(1,128)}, u32[]{:S(2)}) copy-start(s32[1,128]{1,0:T(1,128)} %param.19) | copy-start | bytes 1540
  2.9 55.1 %all-to-all-start = ((f32[4,64,512]{2,1,0:T(8,128)}), f32[4,64,512]{2,1,0:T(8,128)S(1)}, u32[]{:S(2)}, u32[]{:S(2)}) async-start(f32[4,64,512]{2,1,0:T(8,128)} %bitcast), calls=%async_computation | async-start | bytes 1048576 | tf_op jit(solution)/shard_map/all_to_all | solution.py:16
  7.8 49.4 %copy-start.5 = (s32[1,8192]{1,0:T(1,128)S(1)}, s32[1,8192]{1,0:T(1,128)}, u32[]{:S(2)}) copy-start(s32[1,8192]{1,0:T(1,128)} %param.18) | copy-start | bytes 98308
  67.5 23.3 %copy-start.8 = (s32[512]{0:T(512)S(1)}, s32[512]{0:T(512)}, u32[]{:S(2)}) copy-start(s32[512]{0:T(512)} %param.17) | copy-start | bytes 6148
  67.5 23.3 %copy-start.6 = (s32[16,512]{1,0:T(8,128)S(1)}, s32[16,512]{1,0:T(8,128)}, u32[]{:S(2)}) copy-start(s32[16,512]{1,0:T(8,128)} %param.16) | copy-start | bytes 98308
  67.5 58.1 %copy-start.7 = (bf16[256,256]{1,0:T(8,128)(2,1)S(1)}, bf16[256,256]{1,0:T(8,128)(2,1)}, u32[]{:S(2)}) copy-start(bf16[256,256]{1,0:T(8,128)(2,1)} %param.14) | copy-start | bytes 393220
  72.2 53.6 %all-to-all-start.1 = ((bf16[128,2,2048]{2,1,0:T(2,128)(2,1)}), bf16[128,2,2048]{2,1,0:T(2,128)(2,1)S(1)}, u32[]{:S(2)}, u32[]{:S(2)}) async-start(bf16[128,2,2048]{2,1,0:T(2,128)(2,1)} %reshape.115), calls=%async_computation.1 | async-start | bytes 2097152 | tf_op jit(solution)/shard_map/all_to_all | solution.py:50
  129.9 3.4 %copy-start.2 = (s32[16,2,256]{2,1,0:T(2,128)S(1)}, s32[16,2,256]{2,1,0:T(2,128)}, u32[]{:S(2)}) copy-start(s32[16,2,256]{2,1,0:T(2,128)} %reshape.95) | copy-start | bytes 98308
  129.9 3.5 %copy-start.3 = (f32[2,64,256]{2,1,0:T(8,128)S(1)}, f32[2,64,256]{2,1,0:T(8,128)}, u32[]{:S(2)}) copy-start(f32[2,64,256]{2,1,0:T(8,128)} %custom-call.3) | copy-start | bytes 393220
  133.4 43.0 %copy-start.4 = (bf16[256,256]{1,0:T(8,128)(2,1)S(1)}, bf16[256,256]{1,0:T(8,128)(2,1)}, u32[]{:S(2)}) copy-start(bf16[256,256]{1,0:T(8,128)(2,1)} %param.15) | copy-start | bytes 393220
where the time goes:
time: 178 us; the launch traced here: 177 us
  local copies, waits for them, and re-layouts  68.3 us (38%)
  blocking collectives  48.5 us (27%)
  matrix products  35.4 us (20%)
  starting transfers between devices  23.4 us (13%)
    gather x2, local copies, waits for them, and re-layouts, local(): live = lane % capacity < send_count[0][lane // capacity]  48.9 us
    all_gather x1, blocking collectives, local(): lax.all_gather(hidden, 'cols', axis=0, tiled=True)  34.1 us
    dot_general x2, matrix products, aggregate(): return jnp.dot(table, counts, preferred_element_type=jnp.float32)  28 us
    all_to_all x1, starting transfers between devices, local(): lax.all_to_all(outgoing, 'dom', split_axis=1, concat_axis=1, tiled=True)  18.5 us
    all_gather x1, blocking collectives, local(): lax.all_gather(mean, 'cols', axis=0, tiled=True)  14.5 us
    all_to_all x4, local copies, waits for them, and re-layouts, local(): lax.all_to_all(outgoing, 'dom', split_axis=1, concat_axis=1, tiled=True)  10.1 us
    unnamed x21, local copies, waits for them, and re-layouts  7.61 us
    all_to_all x1, starting transfers between devices, sent_and_summed(): blocks = lax.all_to_all(cut_along(shard, dim, size), axis, 0, 0, tiled=True)  4.87 us
  transfers between devices with their start and end apart: 2, of which 0 were waited for; matrix products, arithmetic and copies ran while one was open for 29% of the time, Pallas kernels for 0%

commit v1 on v0

v1 whole, which is shorter than its diff:
```python
import jax
import jax.numpy as jnp
from jax import lax
from jax.experimental import pallas as pl
from jax.experimental.pallas import tpu as pltpu
from jax.sharding import PartitionSpec as P

F32 = jnp.float32
BF16 = jnp.bfloat16
VMEM = pl.BlockSpec(memory_space=pltpu.VMEM)
LIMIT = pltpu.CompilerParams(vmem_limit_bytes=24 * 1024 * 1024)
CAP = 64
HALF = CAP // 2


def cost(flops, nbytes):
    return pl.CostEstimate(flops=flops, bytes_accessed=nbytes, transcendentals=0)


def dot(left, right, dims):
    return lax.dot_general(left, right, (dims, ((), ())), preferred_element_type=F32)


def partial_kernel(features, proj, weight, out):
    joined = dot(weight[...], proj[...], ((0,), (1,)))
    high = joined.astype(BF16)
    low = (joined - high.astype(F32)).astype(BF16)
    wide = dot(high, features[...], ((1,), (0,))) + dot(low, features[...], ((1,), (0,)))
    out[...] = wide.astype(out.dtype)


def partials(features, proj, weight, dtype):
    width, nodes = weight.shape[1], features.shape[1]
    return pl.pallas_call(
        partial_kernel,
        out_shape=jax.ShapeDtypeStruct((width, nodes), dtype),
        in_specs=[VMEM] * 3,
        out_specs=VMEM,
        compiler_params=LIMIT,
        cost_estimate=cost(2 * width * nodes * 640, 1 << 20),
    )(features, proj, weight)


def select_kernel(table, wanted, out):
    width, nodes = table.shape
    columns = wanted.shape[1]
    step = 256
    iota = lax.broadcasted_iota(jnp.int32, (256, step), 0).astype(F32).astype(BF16)
    for start in range(0, columns, step):
        halves = []
        for h in range(2):
            codes = wanted[pl.ds(h, 1), pl.ds(start, step)]
            total = jnp.zeros((width, step), F32)
            for base in range(0, nodes, 256):
                inside = jnp.logical_and(codes >= base, codes < base + 256)
                low = jnp.where(inside, codes - base, -1).astype(F32)
                low = jnp.broadcast_to(low, (16, step)).astype(BF16)
                low = jnp.broadcast_to(low[None], (16, 16, step)).reshape(256, step)
                onehot = jnp.where(iota == low, jnp.ones((), BF16), jnp.zeros((), BF16))
                total = total + dot(table[:, pl.ds(base, 256)], onehot, ((1,), (0,)))
            halves.append(total)
        out[pl.ds(start, step), :] = jnp.concatenate(halves, axis=0).T.astype(BF16)


def select(table, wanted):
    width, nodes = table.shape
    columns = wanted.shape[1]
    return pl.pallas_call(
        select_kernel,
        out_shape=jax.ShapeDtypeStruct((columns, 2 * width), BF16),
        in_specs=[VMEM] * 2,
        out_specs=VMEM,
        compiler_params=LIMIT,
        cost_estimate=cost(2 * width * nodes * 2 * columns, 1 << 20),
    )(table, wanted)


def count_kernel(codes, out, spread):
    slots, nodes = codes.shape
    rows = 64
    iota = lax.broadcasted_iota(jnp.int32, (rows // 16, 16, nodes), 0) * 16
    iota = iota + lax.broadcasted_iota(jnp.int32, (rows // 16, 16, nodes), 1)
    iota = iota.astype(F32).astype(BF16)
    one, zero = jnp.ones((), BF16), jnp.zeros((), BF16)

    def block(b, carry):
        low = codes[...] - b * 256
        low = jnp.where(jnp.logical_and(low >= 0, low < 256), low, -1).astype(F32)
        for k in range(slots):
            spread[k] = jnp.broadcast_to(low[k : k + 1], (16, nodes)).astype(BF16)
        for part in range(256 // rows):
            places = iota + jnp.asarray(part * rows, BF16)
            total = jnp.zeros((rows // 16, 16, nodes), BF16)
            for k in range(slots):
                total = total + jnp.where(places == spread[k][None], one, zero)
            out[pl.ds(b * 16 + part * (rows // 16), rows // 16)] = total
        return carry

    lax.fori_loop(0, out.shape[0] // 16, block, 0)


def count(codes, rows):
    slots, nodes = codes.shape
    counts = pl.pallas_call(
        count_kernel,
        out_shape=jax.ShapeDtypeStruct((rows // 16, 16, nodes), BF16),
        in_specs=[VMEM],
        out_specs=VMEM,
        scratch_shapes=[pltpu.VMEM((slots, 16, nodes), BF16)],
        compiler_params=LIMIT,
        cost_estimate=cost(2 * 10**10, 60 << 20),
    )(codes)
    return counts.reshape(rows, nodes)


def combine_kernel(table, rows, counts, own, degree, out):
    width, nodes = table.shape
    depth = rows.shape[0]
    turned = rows[...].astype(F32).T.astype(BF16)
    total = dot(table[...], counts[pl.ds(0, nodes), :], ((1,), (0,)))
    for h in range(2):
        part = counts[pl.ds(nodes + h * depth, depth), :]
        total = total + dot(turned[h * width : (h + 1) * width], part, ((1,), (0,)))
    result = own[...] + total / degree[...].astype(F32)
    out[...] = jnp.maximum(result, 0.0).astype(BF16)


def combine(table, rows, counts, own, degree):
    width, nodes = table.shape
    return pl.pallas_call(
        combine_kernel,
        out_shape=jax.ShapeDtypeStruct((width, nodes), BF16),
        in_specs=[VMEM] * 5,
        out_specs=VMEM,
        compiler_params=LIMIT,
        cost_estimate=cost(2 * width * nodes * 8704, 10 << 20),
    )(table, rows, counts, own, degree)


def local(features, proj_in, self_weight, neigh_weight, neighbors, degree, send_rows, send_count):
    slots, nodes = neighbors.shape

    sent = partials(features, proj_in, neigh_weight, BF16)
    width = sent.shape[0] // lax.axis_size("cols")
    sent = lax.all_to_all(sent.reshape(-1, width, nodes), "cols", 0, 0, tiled=True)

    live = jnp.arange(CAP, dtype=jnp.int32)[None, :] < send_count[0][:, None]
    wanted = jnp.where(live, send_rows[0].reshape(-1, CAP), -1)
    wanted = jnp.transpose(wanted.reshape(-1, 2, HALF), (1, 0, 2)).reshape(2, -1)

    used = jnp.arange(slots, dtype=jnp.int32)[:, None] < degree[None, :]
    code = neighbors - nodes
    part, slot = code >> 6, code & (CAP - 1)
    remote = nodes + (slot >> 5) * wanted.shape[1] + part * HALF + (slot & (HALF - 1))
    codes = jnp.where(used, jnp.where(code >= 0, remote, neighbors), -1)

    table = jnp.sum(sent.astype(F32), axis=0).astype(BF16)
    own = partials(features, proj_in, self_weight, F32)
    own = lax.psum_scatter(own, "cols", scatter_dimension=0, tiled=True)

    blocks = select(table, wanted).reshape(-1, HALF, 2 * width)
    rows = lax.all_to_all(blocks, "dom", 0, 0, tiled=True).reshape(-1, 2 * width)
    counts = count(codes, nodes + 2 * wanted.shape[1])
    return combine(table, rows, counts, own, degree[None, :])


def solution(mesh):
    return jax.shard_map(
        local,
        mesh=mesh,
        in_specs=(
            P("cols", "dom"),
            P("cols", None),
            P(),
            P(),
            P(None, "dom"),
            P("dom"),
            P("dom", None),
            P("dom", None),
        ),
        out_specs=P("cols", "dom"),
        check_vma=False,
    )
```

time: 178 us -> 96.2 us (0.54)
  the two profiles are of different devices: /device:TPU:2 before, /device:TPU:17 now
where the time goes in v1:
time: 96.2 us; the launch traced here: 95.6 us
  starting transfers between devices  23.8 us (25%)
  Pallas kernels  22.7 us (24%)
  waiting for transfers between devices  18.4 us (19%)
  local copies, waits for them, and re-layouts  14.1 us (15%)
  between operations  13.5 us (14%)
  other arithmetic  3.16 us (3%)
    all_to_all x1, starting transfers between devices, local(): lax.all_to_all(blocks, 'dom', 0, 0, tiled=True).reshape(-1, 2 * width)  19.1 us
    all_to_all x1, waiting for transfers between devices, local(): lax.all_to_all(blocks, 'dom', 0, 0, tiled=True).reshape(-1, 2 * width)  18.4 us
    pallas_call x1, Pallas kernels, count(): pl.pallas_call(count_kernel, out_shape=jax.ShapeDtypeStruct((rows // 16,...  15.2 us
    unnamed x21, local copies, waits for them, and re-layouts  13.8 us
    all_to_all x1, starting transfers between devices, local(): lax.all_to_all(sent.reshape(-1, width, nodes), 'cols', 0, 0, tiled=True)  4.64 us
    pallas_call x1, Pallas kernels, select(): pl.pallas_call(select_kernel, out_shape=jax.ShapeDtypeStruct((columns, 2...  2.66 us
    pallas_call x2, Pallas kernels, partials(): pl.pallas_call(partial_kernel, out_shape=jax.ShapeDtypeStruct((width, nod...  2.51 us
    pallas_call x1, Pallas kernels, combine(): pl.pallas_call(combine_kernel, out_shape=jax.ShapeDtypeStruct((width, nod...  2.34 us
  transfers between devices with their start and end apart: 3, of which 1 were waited for; matrix products, arithmetic and copies ran while one was open for 4% of the time, Pallas kernels for 20%

profile of v1, /device:TPU:17, one launch (start us, length us, event | category | flops | bytes accessed | tf_op | source)
XLA Modules:
  0.0 95.6 jit_solution(13729003929195446956)
XLA Ops:
  6.5 0.0 copy-start.2
  6.5 0.9 copy-done.2
  7.5 0.0 copy-start.4
  7.5 0.9 copy-done.4
  8.4 0.0 copy-start.7
  8.4 0.9 copy-done.7
  9.3 1.2 %shard_map.82 = bf16[256,512]{1,0:T(8,128)(2,1)} custom-call(bf16[192,512]{1,0:T(8,128)(2,1)S(1)} %copy-done.2, bf16[192,256]{1,0:T(8,128)(2,1)S(1)} %copy-done.4, bf16[256,256]{1,0:T(8,128)(2,1)S(1)} %copy-done.7), custom_call_target="tpu_custom_call" | custom-call | flops 167772160 | bytes 1048576 | tf_op jit(solution)/shard_map/pallas_call | solution.py:34
  10.5 4.6 %all-to-all-start = ((bf16[4,64,512]{2,1,0:T(8,128)(2,1)}), bf16[4,64,512]{2,1,0:T(8,128)(2,1)S(1)}, u32[]{:S(2)}, u32[]{:S(2)}) async-start(bf16[4,64,512]{2,1,0:T(8,128)(2,1)} %bitcast), calls=%async_computation | async-start | bytes 524288 | tf_op jit(solution)/shard_map/all_to_all | solution.py:145
  15.1 0.0 reduce-scatter.2.cloned.1.call-start
  15.1 0.0 copy-start.3
  15.1 0.9 copy-done.3
  16.0 0.0 copy-start.5
  16.0 0.9 copy-done.5
  16.9 0.0 copy-start.8
  16.9 0.9 copy-done.8
  17.8 1.3 %shard_map.85 = f32[256,512]{1,0:T(8,128)} custom-call(bf16[192,512]{1,0:T(8,128)(2,1)S(1)} %copy-done.3, bf16[192,256]{1,0:T(8,128)(2,1)S(1)} %copy-done.5, bf16[256,256]{1,0:T(8,128)(2,1)S(1)} %copy-done.8), custom_call_target="tpu_custom_call" | custom-call | flops 167772160 | bytes 1048576 | tf_op jit(solution)/shard_map/pallas_call | solution.py:34
  19.1 0.0 reduce-scatter.2.cloned.1.call-update
  19.2 0.5 broadcast.25
  19.7 1.5 %reduce.4 = s32[8192]{0:T(1024)S(1)} reduce(s32[1,8192]{1,0:T(1,128)} %param.14, s32[]{:T(128)} %broadcast.25), dimensions={0}, to_apply=%param.14.reduce_sub_computation.3 | reduce | bytes 65540 | tf_op args[6]
  21.2 0.1 reshape_squeeze.3
  21.3 0.9 fusion
  22.2 0.1 reshape.34.wanted
  22.3 0.0 all-to-all-done
  22.4 2.7 %shard_map.83 = bf16[4096,128]{1,0:T(8,128)(2,1)} custom-call(bf16[64,512]{1,0:T(8,128)(2,1)S(1)} %reduce_sum.12.table, s32[2,4096]{1,0:T(2,128)S(1)} %reshape.34.wanted), custom_call_target="tpu_custom_call" | custom-call | flops 536870912 | bytes 1048576 | tf_op jit(solution)/shard_map/pallas_call | solution.py:68
  25.1 19.1 %all-to-all-start.1 = ((bf16[128,32,128]{2,1,0:T(8,128)(2,1)}), bf16[128,32,128]{2,1,0:T(8,128)(2,1)S(1)}, u32[]{:S(2)}, u32[]{:S(2)}) async-start(bf16[128,32,128]{2,1,0:T(8,128)(2,1)} %bitcast.3), calls=%async_computation.1 | async-start | bytes 2097152 | tf_op jit(solution)/shard_map/all_to_all | solution.py:162
  44.2 0.8 select_select_fusion.codes
  45.0 0.0 copy-start.9
  45.0 15.2 %shard_map.84 = bf16[544,16,512]{2,1,0:T(8,128)(2,1)S(1)} custom-call(s32[16,512]{1,0:T(8,128)S(1)} %select_select_fusion.codes), custom_call_target="tpu_custom_call" | custom-call | flops 20000000000 | bytes 62914560 | tf_op jit(solution)/shard_map/pallas_call | solution.py:104
  60.2 0.0 copy-start
  60.2 3.4 %copy-done = bf16[544,16,512]{2,1,0:T(8,128)(2,1)} copy-done((bf16[544,16,512]{2,1,0:T(8,128)(2,1)}, bf16[544,16,512]{2,1,0:T(8,128)(2,1)S(1)}, u32[]{:S(2)}) %copy-start) | copy-done | bytes 8912920
  63.6 0.0 reduce-scatter.2.cloned.1.call-done.own
  63.6 18.4 %all-to-all-done.1 = bf16[128,32,128]{2,1,0:T(8,128)(2,1)S(1)} async-done(((bf16[128,32,128]{2,1,0:T(8,128)(2,1)}), bf16[128,32,128]{2,1,0:T(8,128)(2,1)S(1)}, u32[]{:S(2)}, u32[]{:S(2)}) %all-to-all-start.1) | async-done | bytes 1048608 | tf_op jit(solution)/shard_map/all_to_all | solution.py:162
  82.0 0.0 copy-done.9
  82.0 0.0 copy-start.1
  82.0 3.5 %copy-done.1 = bf16[544,16,512]{2,1,0:T(8,128)(2,1)S(1)} copy-done((bf16[544,16,512]{2,1,0:T(8,128)(2,1)S(1)}, bf16[544,16,512]{2,1,0:T(8,128)(2,1)}, u32[]{:S(2)}) %copy-start.1) | copy-done | bytes 8912920
  85.5 0.0 copy-start.6
  85.5 0.9 copy-done.6
  86.4 2.3 %shard_map.86 = bf16[64,512]{1,0:T(8,128)(2,1)} custom-call(bf16[64,512]{1,0:T(8,128)(2,1)S(1)} %reduce_sum.12.table, bf16[4096,128]{1,0:T(8,128)(2,1)S(1)} %bitcast.9, bf16[8704,512]{1,0:T(8,128)(2,1)S(1)} %bitcast.8, f32[64,512]{1,0:T(8,128)S(1)} %copy-done.6, s32[1,512]{1,0:T(1,128)S(1)} %bitcast.10), custom_call_target="tpu_custom_call" | custom-call | flops 570425344 | bytes 10485760 | tf_op jit(solution)/shard_map/pallas_call | solution.py:130
  (3 shorter events, 0.1 us)
Async XLA Ops:
  6.5 0.9 copy-start.2
  7.5 0.9 copy-start.4
  8.4 0.9 copy-start.7
  10.5 11.9 %all-to-all-start = ((bf16[4,64,512]{2,1,0:T(8,128)(2,1)}), bf16[4,64,512]{2,1,0:T(8,128)(2,1)S(1)}, u32[]{:S(2)}, u32[]{:S(2)}) async-start(bf16[4,64,512]{2,1,0:T(8,128)(2,1)} %bitcast), calls=%async_computation | async-start | bytes 524288 | tf_op jit(solution)/shard_map/all_to_all | solution.py:145
  15.1 48.5 %reduce-scatter.2.cloned.1.call-start = ((), (), s32[]{:S(2)}) async-start(), calls=%async_computation.3 | async-start | bytes 655360 | tf_op jit(solution)/shard_map/reduce_scatter | solution.py:159
  15.1 0.9 copy-start.3
  16.0 0.9 copy-start.5
  16.9 0.9 copy-start.8
  25.1 56.9 %all-to-all-start.1 = ((bf16[128,32,128]{2,1,0:T(8,128)(2,1)}), bf16[128,32,128]{2,1,0:T(8,128)(2,1)S(1)}, u32[]{:S(2)}, u32[]{:S(2)}) async-start(bf16[128,32,128]{2,1,0:T(8,128)(2,1)} %bitcast.3), calls=%async_computation.1 | async-start | bytes 2097152 | tf_op jit(solution)/shard_map/all_to_all | solution.py:162
  45.0 37.0 %copy-start.9 = (s32[512]{0:T(512)S(1)}, s32[512]{0:T(512)}, u32[]{:S(2)}) copy-start(s32[512]{0:T(512)} %param.13) | copy-start | bytes 6148
  60.2 3.4 %copy-start = (bf16[544,16,512]{2,1,0:T(8,128)(2,1)}, bf16[544,16,512]{2,1,0:T(8,128)(2,1)S(1)}, u32[]{:S(2)}) copy-start(bf16[544,16,512]{2,1,0:T(8,128)(2,1)S(1)} %shard_map.84) | copy-start | bytes 26738692
  82.0 3.5 %copy-start.1 = (bf16[544,16,512]{2,1,0:T(8,128)(2,1)S(1)}, bf16[544,16,512]{2,1,0:T(8,128)(2,1)}, u32[]{:S(2)}) copy-start(bf16[544,16,512]{2,1,0:T(8,128)(2,1)} %copy-done) | copy-start | bytes 26738692
  85.5 0.9 copy-start.6
Sparse Core Ops, SparseCore 0:
  19.3 31.6 reduce-scatter.1

commit v2 on v1

v2 whole, which is shorter than its diff:
```python
import functools

import jax
import jax.numpy as jnp
from jax import lax
from jax.experimental import pallas as pl
from jax.experimental.pallas import tpu as pltpu
from jax.sharding import Mesh, PartitionSpec as P

F32 = jnp.float32
BF16 = jnp.bfloat16
VMEM = pl.BlockSpec(memory_space=pltpu.VMEM)
LIMIT = pltpu.CompilerParams(vmem_limit_bytes=24 * 1024 * 1024)
PLANE = ("z", "x", "core")
DOM = ("z", "yh", "x", "core")
CAP = 64
HALF = CAP // 2


def cost(flops, nbytes):
    return pl.CostEstimate(flops=flops, bytes_accessed=nbytes, transcendentals=0)


def dot(left, right, dims):
    return lax.dot_general(left, right, (dims, ((), ())), preferred_element_type=F32)


def partial_kernel(turn, features_hbm, proj_hbm, weight_hbm, out, features, proj, weight, wide, arrived):
    copies = [
        pltpu.make_async_copy(source, target, arrived.at[i])
        for i, (source, target) in enumerate(
            ((weight_hbm, weight), (proj_hbm, proj), (features_hbm, features))
        )
    ]
    for copy in copies:
        copy.start()
    copies[0].wait()
    copies[1].wait()
    joined = dot(weight[...], proj[...], ((0,), (1,)))
    high = joined.astype(BF16)
    low = (joined - high.astype(F32)).astype(BF16)
    copies[2].wait()
    total = dot(high, features[...], ((1,), (0,))) + dot(low, features[...], ((1,), (0,)))
    if not turn:
        out[...] = total.astype(out.dtype)
        return
    wide[...] = total
    blocks = lax.axis_size("cols")
    depth = total.shape[0] // blocks
    me = lax.axis_index("cols")
    for s in range(blocks):
        start = pl.multiple_of(lax.rem(me + s, blocks) * depth, depth)
        out[pl.ds(s * depth, depth), :] = wide[pl.ds(start, depth), :].astype(out.dtype)


def partials(features, proj, weight, dtype, turn):
    width, nodes = weight.shape[1], features.shape[1]
    return pl.pallas_call(
        functools.partial(partial_kernel, turn),
        out_shape=jax.ShapeDtypeStruct((width, nodes), dtype),
        in_specs=[pl.BlockSpec(memory_space=pl.ANY)] * 3,
        out_specs=VMEM,
        scratch_shapes=[
            pltpu.VMEM(features.shape, BF16),
            pltpu.VMEM(proj.shape, BF16),
            pltpu.VMEM(weight.shape, BF16),
            pltpu.VMEM((width, nodes), F32),
            pltpu.SemaphoreType.DMA((3,)),
        ],
        compiler_params=LIMIT,
        cost_estimate=cost(2 * width * nodes * 640, 1 << 20),
    )(*(pltpu.with_memory_space_constraint(array, pltpu.HBM) for array in (features, proj, weight)))


def select_kernel(near, far, wanted, out):
    width, nodes = near.shape
    tables = (near, far)
    columns = wanted.shape[2]
    step = 256
    places = step // HALF
    iota = lax.broadcasted_iota(jnp.int32, (256, step), 0).astype(F32).astype(BF16)
    for start in range(0, columns, step):
        for t in range(2):
            halves = []
            for h in range(2):
                codes = wanted[t, pl.ds(h, 1), pl.ds(start, step)]
                total = jnp.zeros((width, step), F32)
                for base in range(0, nodes, 256):
                    inside = jnp.logical_and(codes >= base, codes < base + 256)
                    low = jnp.where(inside, codes - base, -1).astype(F32)
                    low = jnp.broadcast_to(low, (16, step)).astype(BF16)
                    low = jnp.broadcast_to(low[None], (16, 16, step)).reshape(256, step)
                    onehot = jnp.where(iota == low, jnp.ones((), BF16), jnp.zeros((), BF16))
                    total = total + dot(tables[t][:, pl.ds(base, 256)], onehot, ((1,), (0,)))
                halves.append(total)
            rows = jnp.concatenate(halves, axis=0).T.astype(BF16).reshape(places, HALF, 2 * width)
            out[pl.ds(start // HALF, places), pl.ds(t * HALF, HALF), :] = rows


def select(near, far, wanted):
    width, nodes = near.shape
    columns = wanted.shape[2]
    return pl.pallas_call(
        select_kernel,
        out_shape=jax.ShapeDtypeStruct((columns // HALF, CAP, 2 * width), BF16),
        in_specs=[VMEM] * 3,
        out_specs=VMEM,
        compiler_params=LIMIT,
        cost_estimate=cost(8 * width * nodes * columns, 1 << 20),
    )(near, far, wanted)


def count_kernel(first, codes, out, spread, stage, left):
    slots, nodes = codes.shape
    rows = 64
    blocks = out.shape[0] // 16
    iota = lax.broadcasted_iota(jnp.int32, (rows // 16, 16, nodes), 0) * 16
    iota = iota + lax.broadcasted_iota(jnp.int32, (rows // 16, 16, nodes), 1)
    iota = iota.astype(F32).astype(BF16)
    one, zero = jnp.ones((), BF16), jnp.zeros((), BF16)

    def move(b, turn):
        return pltpu.make_async_copy(stage.at[turn], out.at[pl.ds(b * 16, 16)], left.at[turn])

    def block(b, carry):
        turn = lax.rem(b, 2)

        @pl.when(b >= 2)
        def _():
            move(b - 2, turn).wait()

        low = codes[...] - (first + b) * 256
        low = jnp.where(jnp.logical_and(low >= 0, low < 256), low, -1).astype(F32)
        for k in range(slots):
            spread[k] = jnp.broadcast_to(low[k : k + 1], (16, nodes)).astype(BF16)
        for part in range(256 // rows):
            places = iota + jnp.asarray(part * rows, BF16)
            total = jnp.zeros((rows // 16, 16, nodes), BF16)
            for k in range(slots):
                total = total + jnp.where(places == spread[k][None], one, zero)
            stage[turn, pl.ds(part * (rows // 16), rows // 16)] = total
        move(b, turn).start()
        return carry

    lax.fori_loop(0, blocks, block, 0)
    for b in range(blocks - 2, blocks):
        move(b, b % 2).wait()


def count(codes, first, blocks):
    slots, nodes = codes.shape
    counts = pl.pallas_call(
        functools.partial(count_kernel, first),
        out_shape=pltpu.HBM((blocks * 16, 16, nodes), BF16),
        in_specs=[VMEM],
        out_specs=pl.BlockSpec(memory_space=pl.ANY),
        scratch_shapes=[
            pltpu.VMEM((slots, 16, nodes), BF16),
            pltpu.VMEM((2, 16, 16, nodes), BF16),
            pltpu.SemaphoreType.DMA((2,)),
        ],
        compiler_params=LIMIT,
        cost_estimate=cost(blocks * 5 * 10**8, blocks << 20),
    )(codes)
    return counts.reshape(blocks * 256, nodes)


def combine_kernel(splits, table, rows, degree, *refs):
    counts_hbm, refs = refs[: len(splits)], refs[len(splits) :]
    parts, (out, counts, arrived) = refs[:-3], refs[-3:]
    width, nodes = table.shape
    depth = rows.shape[0]
    chunk = 512
    copies = []
    for source, extent in zip(counts_hbm, splits):
        for low in range(0, extent, chunk):
            target = counts.at[pl.ds(len(copies) * chunk, chunk)]
            copy = pltpu.make_async_copy(source.at[pl.ds(low, chunk)], target, arrived.at[len(copies)])
            copy.start()
            copies.append(copy)
    turned = rows[...].astype(F32).T.astype(BF16)
    total = jnp.zeros((width, nodes), F32)
    for i, copy in enumerate(copies):
        start = i * chunk
        if start < nodes:
            left = table[:, start : start + chunk]
        else:
            h, low = divmod(start - nodes, depth)
            left = turned[h * width : (h + 1) * width, low : low + chunk]
        copy.wait()
        total = total + dot(left, counts[pl.ds(start, chunk), :], ((1,), (0,)))
    result = total / degree[...].astype(F32)
    for part in parts:
        result = result + part[...]
    out[...] = jnp.maximum(result, 0.0).astype(BF16)


def combine(table, rows, degree, counts, parts):
    width, nodes = table.shape
    splits = [part.shape[0] for part in counts]
    hbm = [pltpu.with_memory_space_constraint(part, pltpu.HBM) for part in counts]
    return pl.pallas_call(
        functools.partial(combine_kernel, splits),
        out_shape=jax.ShapeDtypeStruct((width, nodes), BF16),
        in_specs=[VMEM] * 3 + [pl.BlockSpec(memory_space=pl.ANY)] * len(hbm) + [VMEM] * len(parts),
        out_specs=VMEM,
        scratch_shapes=[
            pltpu.VMEM((sum(splits), nodes), BF16),
            pltpu.SemaphoreType.DMA((sum(splits) // 512,)),
        ],
        compiler_params=LIMIT,
        cost_estimate=cost(2 * width * nodes * 8704, 10 << 20),
    )(table, rows, degree, *hbm, *parts)


def local(features, proj_in, self_weight, neigh_weight, neighbors, degree, send_rows, send_count):
    slots, nodes = neighbors.shape
    columns = lax.axis_size("cols")
    mine = lax.axis_index("yh")
    swap = [(0, 1), (1, 0)]

    sent = partials(features, proj_in, neigh_weight, BF16, False)
    sent, send_rows, send_count, neighbors = lax.optimization_barrier((sent, send_rows, send_count, neighbors))

    live = jnp.arange(CAP, dtype=jnp.int32)[None, :] < send_count[0][:, None]
    wanted = jnp.where(live, send_rows[0].reshape(-1, CAP), -1)
    wanted = wanted.reshape(lax.axis_size("z"), 2, -1, 2, HALF)
    wanted = jnp.transpose(wanted, (1, 3, 0, 2, 4)).reshape(2, 2, -1)
    here = jnp.where(mine == 0, wanted[0], wanted[1])
    there = jnp.where(mine == 0, wanted[1], wanted[0])
    wanted = jnp.stack([here, lax.ppermute(there, "yh", swap)])
    depth = 2 * wanted.shape[2]

    used = jnp.arange(slots, dtype=jnp.int32)[:, None] < degree[None, :]
    code = neighbors - nodes
    part, slot = code >> 6, code & (CAP - 1)
    place = (part >> 4) * 8 + (part & 7)
    far = ((part >> 3) & 1) ^ mine
    remote = nodes + (slot >> 5) * depth + place * CAP + far * HALF + (slot & (HALF - 1))
    codes = jnp.where(used, jnp.where(code >= 0, remote, neighbors), -1)

    width = sent.shape[0] // columns
    sent = lax.all_to_all(sent.reshape(-1, width, nodes), "cols", 0, 0, tiled=True)
    own = partials(features, proj_in, self_weight, F32, True)

    table = jnp.sum(sent.astype(F32), axis=0).astype(BF16)
    codes, table = lax.optimization_barrier((codes, table))
    partner = lax.ppermute(table, "yh", swap)
    blocks = (nodes + 2 * depth) // 256
    early = blocks // 4 // 2 * 2
    counts = [count(codes, 0, early)]
    wanted, counts[0] = lax.optimization_barrier((wanted, counts[0]))
    chosen = select(table, partner, wanted)
    chosen, own = lax.optimization_barrier((chosen, own))
    rows = lax.all_to_all(chosen, PLANE, 0, 0, tiled=True).reshape(-1, 2 * width)

    parts = [own[:width]]
    for s in range(1, columns):
        ring = [(c, (c + s) % columns) for c in range(columns)]
        parts.append(lax.ppermute(own[s * width : (s + 1) * width], "cols", ring))
    counts.append(count(codes, early, blocks - early))
    return combine(table, rows, degree[None, :], counts, parts)


def solution(mesh):
    fine = Mesh(mesh.devices.reshape(4, 8, 2, 4, 2), ("cols",) + DOM)
    return jax.shard_map(
        local,
        mesh=fine,
        in_specs=(
            P("cols", DOM),
            P("cols", None),
            P(),
            P(),
            P(None, DOM),
            P(DOM),
            P(DOM, None),
            P(DOM, None),
        ),
        out_specs=P("cols", DOM),
        check_vma=False,
    )
```

time: 96.2 us -> 83 us (0.86)
  the two profiles are of different devices: /device:TPU:17 before, /device:TPU:8 now
where the time goes in v2:
time: 83 us; the launch traced here: 82.4 us
  starting transfers between devices  36.6 us (44%)
  Pallas kernels  31.8 us (38%)
  waiting for transfers between devices  9.13 us (11%)
  other arithmetic  3.74 us (5%)
  local copies, waits for them, and re-layouts  0.99 us (1%)
    pallas_call x2, Pallas kernels, count(): pl.pallas_call(functools.partial(count_kernel, first), out_shape=pltpu.HB...  20.6 us
    all_to_all x1, starting transfers between devices, local(): lax.all_to_all(chosen, PLANE, 0, 0, tiled=True).reshape(-1, 2 * width)  11.2 us
    ppermute x3, starting transfers between devices, local(): parts.append(lax.ppermute(own[s * width:(s + 1) * width], 'cols', ring))  11 us
    all_to_all x1, starting transfers between devices, local(): lax.all_to_all(sent.reshape(-1, width, nodes), 'cols', 0, 0, tiled=True)  9.21 us
    ppermute x1, waiting for transfers between devices, local(): wanted = jnp.stack([here, lax.ppermute(there, 'yh', swap)])  4.67 us
    pallas_call x1, Pallas kernels, combine(): pl.pallas_call(functools.partial(combine_kernel, splits), out_shape=jax.S...  4.66 us
    pallas_call x2, Pallas kernels, partials(): pl.pallas_call(functools.partial(partial_kernel, turn), out_shape=jax.Sha...  3.86 us
    optimization_barrier x2, other arithmetic, local(): lax.optimization_barrier((sent, send_rows, send_count, neighbors))  2.8 us
  transfers between devices with their start and end apart: 7, of which 3 were waited for; matrix products, arithmetic and copies ran while one was open for 6% of the time, Pallas kernels for 27%

profile of v2, /device:TPU:8, one launch (start us, length us, event | category | flops | bytes accessed | tf_op | source)
XLA Modules:
  0.0 82.4 jit_solution(3509415861806301008)
XLA Ops:
  0.0 2.3 %shard_map.82 = bf16[256,512]{1,0:T(8,128)(2,1)} custom-call(bf16[192,512]{1,0:T(8,128)(2,1)} %features_hbm.3, bf16[192,256]{1,0:T(8,128)(2,1)} %proj_hbm.3, bf16[256,256]{1,0:T(8,128)(2,1)} %weight_hbm.2), custom_call_target="tpu_custom_call" | custom-call | flops 167772160 | bytes 1048576 | tf_op jit(solution)/shard_map/pallas_call | solution.py:58
  2.3 9.2 %all-to-all-start = ((bf16[4,64,512]{2,1,0:T(8,128)(2,1)}), bf16[4,64,512]{2,1,0:T(8,128)(2,1)S(1)}, u32[]{:S(2)}, u32[]{:S(2)}) async-start(bf16[4,64,512]{2,1,0:T(8,128)(2,1)} %bitcast), calls=%async_computation | async-start | bytes 524288 | tf_op jit(solution)/shard_map/all_to_all | solution.py:243
  11.5 0.5 broadcast.41
  12.0 1.3 %reduce.8 = s32[128]{0:T(128)S(1)} reduce(s32[1,128]{1,0:T(1,128)} %param.15, s32[]{:T(128)} %broadcast.41), dimensions={0}, to_apply=%get-tuple-element.18.reduce_sub_computation.3 | reduce | bytes 1028 | tf_op jit(solution)/shard_map/optimization_barrier | solution.py:223
  13.3 0.1 lt.42
  13.4 1.5 %reduce.7 = s32[8192]{0:T(1024)S(1)} reduce(s32[1,8192]{1,0:T(1,128)} %param.14, s32[]{:T(128)} %broadcast.41), dimensions={0}, to_apply=%get-tuple-element.19.reduce_sub_computation.3 | reduce | bytes 65540 | tf_op jit(solution)/shard_map/optimization_barrier | solution.py:223
  14.9 0.1 reshape_squeeze.3
  15.1 0.1 fusion
  15.2 0.1 select_n.45
  15.3 2.4 %collective-permute-start.1 = (s32[2,2048]{1,0:T(2,128)S(1)}, s32[2,2048]{1,0:T(2,128)S(1)}, u32[]{:S(2)}, u32[]{:S(2)}) collective-permute-start(s32[2,2048]{1,0:T(2,128)S(1)} %select_n.45), channel_id=1, source_target_pairs={{0,8},{8,0},{1,9},{9,1},{2,10},{10,2},{3,11},{11,3},{4,12},{12,4},... | collective-permute-start | bytes 49160 | tf_op jit(solution)/shard_map/ppermute | solution.py:231
  17.6 0.8 select_select_fusion.codes
  18.4 0.1 select_n.43
  18.5 1.6 %shard_map.85 = f32[256,512]{1,0:T(8,128)S(1)} custom-call(bf16[192,512]{1,0:T(8,128)(2,1)} %features_hbm.3, bf16[192,256]{1,0:T(8,128)(2,1)} %proj_hbm.3, bf16[256,256]{1,0:T(8,128)(2,1)} %weight_hbm.3), custom_call_target="tpu_custom_call" | custom-call | flops 167772160 | bytes 1048576 | tf_op jit(solution)/shard_map/pallas_call | solution.py:58
  20.1 4.7 %collective-permute-done.1 = s32[2,2048]{1,0:T(2,128)S(1)} collective-permute-done((s32[2,2048]{1,0:T(2,128)S(1)}, s32[2,2048]{1,0:T(2,128)S(1)}, u32[]{:S(2)}, u32[]{:S(2)}) %collective-permute-start.1) | collective-permute-done | bytes 16416 | tf_op jit(solution)/shard_map/ppermute | solution.py:231
  24.8 0.0 all-to-all-done
  24.9 2.8 %collective-permute-start = (bf16[64,512]{1,0:T(8,128)(2,1)S(1)}, bf16[64,512]{1,0:T(8,128)(2,1)S(1)}, u32[]{:S(2)}, u32[]{:S(2)}) collective-permute-start(bf16[64,512]{1,0:T(8,128)(2,1)S(1)} %reduce_sum.12.near.table), channel_id=1, source_target_pairs={{0,8},{8,0},{1,9},{9,1},{2,10},{10,2},{3,11},{11,3},{4,12},{12,4},... | collective-permute-start | bytes 196616 | tf_op jit(solution)/shard_map/ppermute | solution.py:248
  27.6 5.1 %shard_map.83 = bf16[128,16,512]{2,1,0:T(8,128)(2,1)} custom-call(s32[16,512]{1,0:T(8,128)S(1)} %select_select_fusion.codes), custom_call_target="tpu_custom_call" | custom-call | flops 4000000000 | bytes 8388608 | tf_op jit(solution)/shard_map/pallas_call | solution.py:152
  32.8 2.2 %collective-permute-done.far = bf16[64,512]{1,0:T(8,128)(2,1)S(1)} collective-permute-done((bf16[64,512]{1,0:T(8,128)(2,1)S(1)}, bf16[64,512]{1,0:T(8,128)(2,1)S(1)}, u32[]{:S(2)}, u32[]{:S(2)}) %collective-permute-start) | collective-permute-done | bytes 65568 | tf_op jit(solution)/shard_map/ppermute | solution.py:248
  34.9 2.7 %shard_map.84 = bf16[64,64,128]{2,1,0:T(8,128)(2,1)} custom-call(bf16[64,512]{1,0:T(8,128)(2,1)S(1)} %reduce_sum.12.near.table, bf16[64,512]{1,0:T(8,128)(2,1)S(1)} %collective-permute-done.far, s32[2,2,2048]{2,1,0:T(2,128)S(1)} %pad_add_fusion.wanted), custom_call_target="tpu_custom_call" | custom-call | flops 536870912 | bytes 1048576 | tf_op jit(solution)/shard_map/pallas_call | solution.py:103
  37.6 11.2 %all-to-all-start.1 = ((bf16[64,64,128]{2,1,0:T(8,128)(2,1)}), bf16[64,64,128]{2,1,0:T(8,128)(2,1)S(1)}, u32[]{:S(2)}, u32[]{:S(2)}) async-start(bf16[64,64,128]{2,1,0:T(8,128)(2,1)} %shard_map.84), calls=%async_computation.1 | async-start | bytes 2097152 | tf_op jit(solution)/shard_map/all_to_all | solution.py:255
  48.9 2.0 %collective-permute-start.4 = (f32[64,512]{1,0:T(8,128)S(1)}, f32[64,512]{1,0:T(8,128)S(1)}, u32[]{:S(2)}, u32[]{:S(2)}) collective-permute-start(f32[64,512]{1,0:T(8,128)S(1)} %get-tuple-element.25), channel_id=1, source_target_pairs={{0,384},{128,0},{256,128},{384,256},{1,385},{129,1},{257,129},{385... | collective-permute-start | bytes 393224 | tf_op jit(solution)/shard_map/ppermute | solution.py:260
  50.9 4.8 %collective-permute-start.3 = (f32[64,512]{1,0:T(8,128)S(1)}, f32[64,512]{1,0:T(8,128)S(1)}, u32[]{:S(2)}, u32[]{:S(2)}) collective-permute-start(f32[64,512]{1,0:T(8,128)S(1)} %get-tuple-element.26), channel_id=1, source_target_pairs={{0,256},{128,384},{256,0},{384,128},{1,257},{129,385},{257,1},{385... | collective-permute-start | bytes 393224 | tf_op jit(solution)/shard_map/ppermute | solution.py:260
  55.7 0.0 copy-start
  55.7 4.3 %collective-permute-start.2 = (f32[64,512]{1,0:T(8,128)S(1)}, f32[64,512]{1,0:T(8,128)S(1)}, u32[]{:S(2)}, u32[]{:S(2)}) collective-permute-start(f32[64,512]{1,0:T(8,128)S(1)} %get-tuple-element.27), channel_id=1, source_target_pairs={{0,128},{128,256},{256,384},{384,0},{1,129},{129,257},{257,385},{3... | collective-permute-start | bytes 393224 | tf_op jit(solution)/shard_map/ppermute | solution.py:260
  60.0 15.5 %shard_map.86 = bf16[416,16,512]{2,1,0:T(8,128)(2,1)} custom-call(s32[16,512]{1,0:T(8,128)S(1)} %select_select_fusion.codes), custom_call_target="tpu_custom_call" | custom-call | flops 12999999488 | bytes 27262976 | tf_op jit(solution)/shard_map/pallas_call | solution.py:152
  75.4 0.0 collective-permute-done.4.refs_5_
  75.4 0.0 collective-permute-done.3.refs_4_
  75.5 0.0 collective-permute-done.2.refs_3_
  75.5 2.3 %all-to-all-done.1 = bf16[64,64,128]{2,1,0:T(8,128)(2,1)S(1)} async-done(((bf16[64,64,128]{2,1,0:T(8,128)(2,1)}), bf16[64,64,128]{2,1,0:T(8,128)(2,1)S(1)}, u32[]{:S(2)}, u32[]{:S(2)}) %all-to-all-start.1) | async-done | bytes 1048608 | tf_op jit(solution)/shard_map/all_to_all | solution.py:255
  77.8 0.0 copy-done
  77.8 4.7 %shard_map.87 = bf16[64,512]{1,0:T(8,128)(2,1)} custom-call(bf16[64,512]{1,0:T(8,128)(2,1)S(1)} %reduce_sum.12.near.table, bf16[4096,128]{1,0:T(8,128)(2,1)S(1)} %bitcast.12, s32[1,512]{1,0:T(1,128)S(1)} %bitcast.13, bf16[2048,512]{1,0:T(8,128)(2,1)} %bitcast.15, bf16[6656,512]{1,0:T(8,128)(2,1)} %bitcast.14, f32[64,512]{1,0:T(8,128)S(1)} %get-tuple-element.28.refs_2_, ...), custom_call_target="tpu_custom_call" | custom-call | flops 570425344 | bytes 10485760 | tf_op jit(solution)/shard_map/pallas_call | solution.py:202
  (6 shorter events, 0.1 us)
Async XLA Ops:
  2.3 22.6 %all-to-all-start = ((bf16[4,64,512]{2,1,0:T(8,128)(2,1)}), bf16[4,64,512]{2,1,0:T(8,128)(2,1)S(1)}, u32[]{:S(2)}, u32[]{:S(2)}) async-start(bf16[4,64,512]{2,1,0:T(8,128)(2,1)} %bitcast), calls=%async_computation | async-start | bytes 524288 | tf_op jit(solution)/shard_map/all_to_all | solution.py:243
  15.3 9.5 %collective-permute-start.1 = (s32[2,2048]{1,0:T(2,128)S(1)}, s32[2,2048]{1,0:T(2,128)S(1)}, u32[]{:S(2)}, u32[]{:S(2)}) collective-permute-start(s32[2,2048]{1,0:T(2,128)S(1)} %select_n.45), channel_id=1, source_target_pairs={{0,8},{8,0},{1,9},{9,1},{2,10},{10,2},{3,11},{11,3},{4,12},{12,4},... | collective-permute-start | bytes 49160 | tf_op jit(solution)/shard_map/ppermute | solution.py:231
  24.9 10.1 %collective-permute-start = (bf16[64,512]{1,0:T(8,128)(2,1)S(1)}, bf16[64,512]{1,0:T(8,128)(2,1)S(1)}, u32[]{:S(2)}, u32[]{:S(2)}) collective-permute-start(bf16[64,512]{1,0:T(8,128)(2,1)S(1)} %reduce_sum.12.near.table), channel_id=1, source_target_pairs={{0,8},{8,0},{1,9},{9,1},{2,10},{10,2},{3,11},{11,3},{4,12},{12,4},... | collective-permute-start | bytes 196616 | tf_op jit(solution)/shard_map/ppermute | solution.py:248
  37.6 40.1 %all-to-all-start.1 = ((bf16[64,64,128]{2,1,0:T(8,128)(2,1)}), bf16[64,64,128]{2,1,0:T(8,128)(2,1)S(1)}, u32[]{:S(2)}, u32[]{:S(2)}) async-start(bf16[64,64,128]{2,1,0:T(8,128)(2,1)} %shard_map.84), calls=%async_computation.1 | async-start | bytes 2097152 | tf_op jit(solution)/shard_map/all_to_all | solution.py:255
  48.9 26.5 %collective-permute-start.4 = (f32[64,512]{1,0:T(8,128)S(1)}, f32[64,512]{1,0:T(8,128)S(1)}, u32[]{:S(2)}, u32[]{:S(2)}) collective-permute-start(f32[64,512]{1,0:T(8,128)S(1)} %get-tuple-element.25), channel_id=1, source_target_pairs={{0,384},{128,0},{256,128},{384,256},{1,385},{129,1},{257,129},{385... | collective-permute-start | bytes 393224 | tf_op jit(solution)/shard_map/ppermute | solution.py:260
  50.9 24.5 %collective-permute-start.3 = (f32[64,512]{1,0:T(8,128)S(1)}, f32[64,512]{1,0:T(8,128)S(1)}, u32[]{:S(2)}, u32[]{:S(2)}) collective-permute-start(f32[64,512]{1,0:T(8,128)S(1)} %get-tuple-element.26), channel_id=1, source_target_pairs={{0,256},{128,384},{256,0},{384,128},{1,257},{129,385},{257,1},{385... | collective-permute-start | bytes 393224 | tf_op jit(solution)/shard_map/ppermute | solution.py:260
  55.7 22.1 %copy-start = (s32[512]{0:T(512)S(1)}, s32[512]{0:T(512)}, u32[]{:S(2)}) copy-start(s32[512]{0:T(512)} %param.13) | copy-start | bytes 6148
  55.7 19.8 %collective-permute-start.2 = (f32[64,512]{1,0:T(8,128)S(1)}, f32[64,512]{1,0:T(8,128)S(1)}, u32[]{:S(2)}, u32[]{:S(2)}) collective-permute-start(f32[64,512]{1,0:T(8,128)S(1)} %get-tuple-element.27), channel_id=1, source_target_pairs={{0,128},{128,256},{256,384},{384,0},{1,129},{129,257},{257,385},{3... | collective-permute-start | bytes 393224 | tf_op jit(solution)/shard_map/ppermute | solution.py:260

commit v3 on v1

v3 whole, which is shorter than its diff:
```python
import functools

import jax
import jax.numpy as jnp
from jax import lax
from jax.experimental import pallas as pl
from jax.experimental.pallas import tpu as pltpu
from jax.sharding import PartitionSpec as P

F32 = jnp.float32
BF16 = jnp.bfloat16
F8 = jnp.float8_e4m3fn
VMEM = pl.BlockSpec(memory_space=pltpu.VMEM)
LIMIT = pltpu.CompilerParams(vmem_limit_bytes=24 * 1024 * 1024)
CAP = 64
PACK, BITS = 6, 5
HALF = CAP // 2


def cost(flops, nbytes):
    return pl.CostEstimate(flops=flops, bytes_accessed=nbytes, transcendentals=0)


def dot(left, right, dims):
    return lax.dot_general(left, right, (dims, ((), ())), preferred_element_type=F32)


def partial_kernel(turn, features_hbm, proj_hbm, weight_hbm, out, features, proj, weight, wide, arrived):
    pairs = ((proj_hbm, proj), (weight_hbm, weight), (features_hbm, features))
    copies = [pltpu.make_async_copy(*pair, arrived.at[i]) for i, pair in enumerate(pairs)]
    for copy in copies:
        copy.start()
    copies[0].wait()
    copies[1].wait()
    joined = dot(weight[...], proj[...], ((0,), (1,)))
    high = joined.astype(BF16)
    low = (joined - high.astype(F32)).astype(BF16)
    copies[2].wait()
    total = dot(high, features[...], ((1,), (0,))) + dot(low, features[...], ((1,), (0,)))
    columns, depth = out.shape[0], out.shape[1]
    if not turn:
        out[...] = total.astype(BF16).reshape(out.shape)
        return
    wide[...] = total
    me = lax.axis_index("cols")
    for s in range(columns):
        start = pl.multiple_of(lax.rem(me + s, columns) * depth, depth)
        out[s] = wide[pl.ds(start, depth), :].astype(BF16)


def partials(features, proj, weight, columns, turn):
    width, nodes = weight.shape[1], features.shape[1]
    arrays = (features, proj, weight)
    return pl.pallas_call(
        functools.partial(partial_kernel, turn),
        out_shape=jax.ShapeDtypeStruct((columns, width // columns, nodes), BF16),
        in_specs=[pl.BlockSpec(memory_space=pl.ANY)] * 3,
        out_specs=VMEM,
        scratch_shapes=[pltpu.VMEM(array.shape, BF16) for array in arrays]
        + [pltpu.VMEM((width, nodes), F32), pltpu.SemaphoreType.DMA((3,))],
        compiler_params=LIMIT,
        cost_estimate=cost(2 * width * nodes * 640, 1 << 20),
    )(*(pltpu.with_memory_space_constraint(array, pltpu.HBM) for array in arrays))


def select_kernel(sent, wanted, rows, table):
    width, nodes = table.shape
    total = sent[0].astype(F32)
    for c in range(1, sent.shape[0]):
        total = total + sent[c].astype(F32)
    table[...] = total.astype(BF16)
    step = 256
    iota = lax.broadcasted_iota(jnp.int32, (256, step), 0).astype(F32).astype(BF16)
    for start in range(0, wanted.shape[1], step):
        halves = []
        for h in range(2):
            codes = wanted[pl.ds(h, 1), pl.ds(start, step)]
            picked = jnp.zeros((width, step), F32)
            for base in range(0, nodes, 256):
                inside = jnp.logical_and(codes >= base, codes < base + 256)
                low = jnp.where(inside, codes - base, -1).astype(F32)
                low = jnp.broadcast_to(low, (16, step)).astype(BF16)
                low = jnp.broadcast_to(low[None], (16, 16, step)).reshape(256, step)
                onehot = jnp.where(iota == low, jnp.ones((), BF16), jnp.zeros((), BF16))
                picked = picked + dot(table[:, pl.ds(base, 256)], onehot, ((1,), (0,)))
            halves.append(picked)
        rows[pl.ds(start, step), :] = jnp.concatenate(halves, axis=0).T.astype(BF16)


def select(sent, wanted):
    width, nodes = sent.shape[1], sent.shape[2]
    columns = wanted.shape[1]
    return pl.pallas_call(
        select_kernel,
        out_shape=(
            jax.ShapeDtypeStruct((columns, 2 * width), BF16),
            jax.ShapeDtypeStruct((width, nodes), BF16),
        ),
        in_specs=[VMEM] * 2,
        out_specs=(VMEM,) * 2,
        compiler_params=LIMIT,
        cost_estimate=cost(4 * width * nodes * columns, 1 << 20),
    )(sent, wanted)


def count_kernel(codes, out, spread, stage, left):
    slots, nodes = codes.shape
    block, strip = stage.shape[1] // PACK, 32
    span = PACK * block
    iota = lax.broadcasted_iota(jnp.int32, (strip, nodes), 0)

    def move(i, size, turn):
        return pltpu.make_async_copy(
            stage.at[turn, pl.ds(0, size)], out.at[pl.ds(i * span, size)], left.at[turn]
        )

    def group(i, turn):
        code = codes[...] - i * span
        inside = jnp.logical_and(code >= 0, code < span)
        spread[0] = jnp.where(inside, code & (block - 1), -1)
        spread[1] = jnp.where(inside, 1 << ((code >> 7) * BITS), 0)
        for low in range(0, block, strip):
            places = iota + low
            total = jnp.zeros((strip, nodes), jnp.int32)
            for k in range(slots):
                total = total + jnp.where(places == spread[0, k : k + 1, :], spread[1, k : k + 1, :], 0)
            for j in range(PACK):
                part = (total >> (j * BITS)) & (2**BITS - 1)
                stage[turn, pl.ds(j * block + low, strip), :] = part.astype(F32).astype(out.dtype)

    def step(i, carry):
        turn = lax.rem(i, 2)

        @pl.when(i >= 2)
        def _():
            move(i - 2, span, turn).wait()

        group(i, turn)
        move(i, span, turn).start()
        return carry

    last = pl.cdiv(out.shape[0], span) - 1
    lax.fori_loop(0, last, step, 0)
    move(last - 2, span, last % 2).wait()
    group(last, last % 2)
    move(last, out.shape[0] - last * span, last % 2).start()
    move(last - 1, span, (last - 1) % 2).wait()
    move(last, out.shape[0] - last * span, last % 2).wait()


def count(codes, rows):
    slots, nodes = codes.shape
    return pl.pallas_call(
        count_kernel,
        out_shape=pltpu.HBM((rows, nodes), F8),
        in_specs=[VMEM],
        out_specs=pl.BlockSpec(memory_space=pl.ANY),
        scratch_shapes=[
            pltpu.VMEM((2, slots, nodes), jnp.int32),
            pltpu.VMEM((2, PACK * 128, nodes), F8),
            pltpu.SemaphoreType.DMA((2,)),
        ],
        compiler_params=LIMIT,
        cost_estimate=cost(9 * 10**9, 20 << 20),
    )(codes)


def combine_kernel(table, rows, degree, counts_hbm, *refs):
    parts, (out, counts, arrived) = refs[:-3], refs[-3:]
    width, nodes = table.shape
    depth = rows.shape[0]
    chunk = 512
    copies = []
    for i in range(counts.shape[0] // chunk):
        at = pl.ds(i * chunk, chunk)
        copies.append(pltpu.make_async_copy(counts_hbm.at[at], counts.at[at], arrived.at[i]))
        copies[i].start()
    turned = rows[...].astype(F32).T.astype(BF16)
    total = jnp.zeros((width, nodes), F32)
    for i, copy in enumerate(copies):
        start = i * chunk
        if start < nodes:
            left = table[:, start : start + chunk]
        else:
            h, low = divmod(start - nodes, depth)
            left = turned[h * width : (h + 1) * width, low : low + chunk]
        copy.wait()
        total = total + dot(left, counts[pl.ds(start, chunk), :].astype(BF16), ((1,), (0,)))
    result = total / degree[...].astype(F32)
    for part in parts:
        result = result + part[...].astype(F32)
    out[...] = jnp.maximum(result, 0.0).astype(BF16)


def combine(table, rows, degree, counts, parts):
    width, nodes = table.shape
    return pl.pallas_call(
        combine_kernel,
        out_shape=jax.ShapeDtypeStruct((width, nodes), BF16),
        in_specs=[VMEM] * 3 + [pl.BlockSpec(memory_space=pl.ANY)] + [VMEM] * len(parts),
        out_specs=VMEM,
        scratch_shapes=[pltpu.VMEM(counts.shape, F8), pltpu.SemaphoreType.DMA((counts.shape[0] // 512,))],
        compiler_params=LIMIT,
        cost_estimate=cost(2 * width * nodes * 8704, 10 << 20),
    )(table, rows, degree, pltpu.with_memory_space_constraint(counts, pltpu.HBM), *parts)


def local(features, proj_in, self_weight, neigh_weight, neighbors, degree, send_rows, send_count):
    slots, nodes = neighbors.shape
    columns = lax.axis_size("cols")
    sent = partials(features, proj_in, neigh_weight, columns, False)
    sent, send_rows, send_count, neighbors = lax.optimization_barrier((sent, send_rows, send_count, neighbors))
    sent = lax.all_to_all(sent, "cols", 0, 0, tiled=True)

    live = jnp.arange(CAP, dtype=jnp.int32).reshape(1, 2, HALF) < send_count.reshape(-1, 1, 1)
    wanted = jnp.where(live, send_rows.reshape(-1, 2, HALF), -1)
    wanted = jnp.transpose(wanted, (1, 0, 2)).reshape(2, -1)
    depth = wanted.shape[1]

    used = jnp.arange(slots, dtype=jnp.int32)[:, None] < degree[None, :]
    code = neighbors - nodes
    part, slot = code >> 6, code & (CAP - 1)
    remote = nodes + (slot >> 5) * depth + part * HALF + (slot & (HALF - 1))
    codes = jnp.where(used, jnp.where(code >= 0, remote, neighbors), -1)

    own = partials(features, proj_in, self_weight, columns, True)
    chosen, table = select(sent, wanted)
    chosen, codes, own = lax.optimization_barrier((chosen, codes, own))
    rows = lax.all_to_all(chosen.reshape(-1, HALF, chosen.shape[1]), "dom", 0, 0, tiled=True)
    parts = [own[0]]
    for s in range(1, columns):
        parts.append(lax.ppermute(own[s], "cols", [(c, (c + s) % columns) for c in range(columns)]))
    counts = count(codes, nodes + 2 * depth)
    return combine(table, rows.reshape(chosen.shape), degree[None, :], counts, parts)


def solution(mesh):
    return jax.shard_map(
        local,
        mesh=mesh,
        in_specs=(
            P("cols", "dom"),
            P("cols", None),
            P(),
            P(),
            P(None, "dom"),
            P("dom"),
            P("dom", None),
            P("dom", None),
        ),
        out_specs=P("cols", "dom"),
        check_vma=False,
    )
```

time: 96.2 us -> 75.7 us (0.79)
  the two profiles are of different devices: /device:TPU:17 before, /device:TPU:9 now
where the time goes in v3:
time: 75.7 us; the launch traced here: 75.2 us
  starting transfers between devices  35.3 us (47%)
  Pallas kernels  19.1 us (25%)
  waiting for transfers between devices  16.7 us (22%)
  other arithmetic  3.12 us (4%)
  local copies, waits for them, and re-layouts  0.81 us (1%)
    all_to_all x1, starting transfers between devices, local(): lax.all_to_all(chosen.reshape(-1, HALF, chosen.shape[1]), 'dom', 0, 0, ti...  20.8 us
    ppermute x3, waiting for transfers between devices, local(): lax.ppermute(own[s], 'cols', [(c, (c + s) % columns) for c in range(colum...  10.9 us
    ppermute x3, starting transfers between devices, local(): lax.ppermute(own[s], 'cols', [(c, (c + s) % columns) for c in range(colum...  9.67 us
    pallas_call x1, Pallas kernels, count(): pl.pallas_call(count_kernel, out_shape=pltpu.HBM((rows, nodes), F8), in_s...  8.68 us
    all_to_all x1, waiting for transfers between devices, local(): lax.all_to_all(chosen.reshape(-1, HALF, chosen.shape[1]), 'dom', 0, 0, ti...  5.78 us
    all_to_all x1, starting transfers between devices, local(): sent = lax.all_to_all(sent, 'cols', 0, 0, tiled=True)  4.77 us
    pallas_call x1, Pallas kernels, combine(): pl.pallas_call(combine_kernel, out_shape=jax.ShapeDtypeStruct((width, nod...  3.94 us
    pallas_call x2, Pallas kernels, partials(): pl.pallas_call(functools.partial(partial_kernel, turn), out_shape=jax.Sha...  3.86 us
  transfers between devices with their start and end apart: 5, of which 4 were waited for; matrix products, arithmetic and copies ran while one was open for 5% of the time, Pallas kernels for 14%

profile of v3, /device:TPU:9, one launch (start us, length us, event | category | flops | bytes accessed | tf_op | source)
XLA Modules:
  0.0 75.2 jit_solution(15354948112191257534)
XLA Ops:
  0.0 2.3 %shard_map.82 = bf16[4,64,512]{2,1,0:T(8,128)(2,1)} custom-call(bf16[192,512]{1,0:T(8,128)(2,1)} %features_hbm.3, bf16[192,256]{1,0:T(8,128)(2,1)} %proj_hbm.3, bf16[256,256]{1,0:T(8,128)(2,1)} %weight_hbm.2), custom_call_target="tpu_custom_call" | custom-call | flops 167772160 | bytes 1048576 | tf_op jit(solution)/shard_map/pallas_call | solution.py:54
  2.3 4.8 %all-to-all-start = ((bf16[4,64,512]{2,1,0:T(8,128)(2,1)}), bf16[4,64,512]{2,1,0:T(8,128)(2,1)S(1)}, u32[]{:S(2)}, u32[]{:S(2)}) async-start(bf16[4,64,512]{2,1,0:T(8,128)(2,1)} %shard_map.82), calls=%async_computation | async-start | bytes 524288 | tf_op jit(solution)/shard_map/all_to_all | solution.py:213
  7.0 0.5 broadcast.20
  7.5 1.5 %reduce.3 = s32[8192]{0:T(1024)S(1)} reduce(s32[1,8192]{1,0:T(1,128)} %param.14, s32[]{:T(128)} %broadcast.20), dimensions={0}, to_apply=%get-tuple-element.16.reduce_sub_computation.3 | reduce | bytes 65540 | tf_op jit(solution)/shard_map/optimization_barrier | solution.py:212
  9.0 0.1 reshape.35
  9.2 0.9 %fusion = s32[2,128,32]{2,0,1:T(2,128)S(1)} fusion(s32[128,2,32]{2,1,0:T(2,128)S(1)} %reshape.35, s32[2,32]{1,0:T(2,128)S(1)} %multiply_add_fusion, s32[128]{0:T(128)} %bitcast.16), kind=kLoop, calls=%fused_computation.1 | loop fusion | flops 16384 | bytes 66304 | tf_op jit(solution)/shard_map/transpose | solution.py:217
  10.1 0.1 reshape.36.wanted
  10.2 1.6 %shard_map.84 = bf16[4,64,512]{2,1,0:T(8,128)(2,1)S(1)} custom-call(bf16[192,512]{1,0:T(8,128)(2,1)} %features_hbm.3, bf16[192,256]{1,0:T(8,128)(2,1)} %proj_hbm.3, bf16[256,256]{1,0:T(8,128)(2,1)} %weight_hbm.3), custom_call_target="tpu_custom_call" | custom-call | flops 167772160 | bytes 1048576 | tf_op jit(solution)/shard_map/pallas_call | solution.py:54
  11.8 0.8 %select_select_fusion.codes = s32[16,512]{1,0:T(8,128)S(1)} fusion(s32[16,512]{1,0:T(8,128)} %param.12, s32[512]{0:T(512)} %param.13), kind=kLoop, calls=%fused_computation.6 | loop fusion | flops 114688 | bytes 67584 | tf_op jit(solution)/shard_map/jit(_where)/select_n | solution.py:224
  12.6 0.0 all-to-all-done.sent
  12.6 2.7 %shard_map.83 = (bf16[4096,128]{1,0:T(8,128)(2,1)}, bf16[64,512]{1,0:T(8,128)(2,1)S(1)}) custom-call(bf16[4,64,512]{2,1,0:T(8,128)(2,1)S(1)} %all-to-all-done.sent, s32[2,4096]{1,0:T(2,128)S(1)} %reshape.36.wanted), custom_call_target="tpu_custom_call" | custom-call | flops 536870912 | bytes 1048576 | tf_op jit(solution)/shard_map/pallas_call | solution.py:93
  15.3 20.8 %all-to-all-start.1 = ((bf16[128,32,128]{2,1,0:T(8,128)(2,1)}), bf16[128,32,128]{2,1,0:T(8,128)(2,1)S(1)}, u32[]{:S(2)}, u32[]{:S(2)}) async-start(bf16[128,32,128]{2,1,0:T(8,128)(2,1)} %bitcast.2), calls=%async_computation.1 | async-start | bytes 2097152 | tf_op jit(solution)/shard_map/all_to_all | solution.py:229
  36.1 3.5 %collective-permute-start.2 = (bf16[64,512]{1,0:T(8,128)(2,1)S(1)}, bf16[64,512]{1,0:T(8,128)(2,1)S(1)}, u32[]{:S(2)}, u32[]{:S(2)}) collective-permute-start(bf16[64,512]{1,0:T(8,128)(2,1)S(1)} %get-tuple-element.23), channel_id=1, source_target_pairs={{0,384},{128,0},{256,128},{384,256},{1,385},{129,1},{257,129},{385... | collective-permute-start | bytes 196616 | tf_op jit(solution)/shard_map/ppermute | solution.py:232
  39.7 1.9 %collective-permute-start.1 = (bf16[64,512]{1,0:T(8,128)(2,1)S(1)}, bf16[64,512]{1,0:T(8,128)(2,1)S(1)}, u32[]{:S(2)}, u32[]{:S(2)}) collective-permute-start(bf16[64,512]{1,0:T(8,128)(2,1)S(1)} %get-tuple-element.24), channel_id=1, source_target_pairs={{0,256},{128,384},{256,0},{384,128},{1,257},{129,385},{257,1},{385... | collective-permute-start | bytes 196616 | tf_op jit(solution)/shard_map/ppermute | solution.py:232
  41.6 0.0 copy-start
  41.6 4.2 %collective-permute-start = (bf16[64,512]{1,0:T(8,128)(2,1)S(1)}, bf16[64,512]{1,0:T(8,128)(2,1)S(1)}, u32[]{:S(2)}, u32[]{:S(2)}) collective-permute-start(bf16[64,512]{1,0:T(8,128)(2,1)S(1)} %get-tuple-element.25), channel_id=1, source_target_pairs={{0,128},{128,256},{256,384},{384,0},{1,129},{129,257},{257,385},{3... | collective-permute-start | bytes 196616 | tf_op jit(solution)/shard_map/ppermute | solution.py:232
  45.8 8.7 %shard_map.85.counts_hbm = f8e4m3fn[8704,512]{1,0:T(32,128)(4,1)} custom-call(s32[16,512]{1,0:T(8,128)S(1)} %select_select_fusion.codes), custom_call_target="tpu_custom_call" | custom-call | flops 8999999488 | bytes 20971520 | tf_op jit(solution)/shard_map/pallas_call | solution.py:153
  54.5 5.1 %collective-permute-done.2.refs_3_ = bf16[64,512]{1,0:T(8,128)(2,1)S(1)} collective-permute-done((bf16[64,512]{1,0:T(8,128)(2,1)S(1)}, bf16[64,512]{1,0:T(8,128)(2,1)S(1)}, u32[]{:S(2)}, u32[]{:S(2)}) %collective-permute-start.2) | collective-permute-done | bytes 65568 | tf_op jit(solution)/shard_map/ppermute | solution.py:232
  59.7 4.1 %collective-permute-done.1.refs_2_ = bf16[64,512]{1,0:T(8,128)(2,1)S(1)} collective-permute-done((bf16[64,512]{1,0:T(8,128)(2,1)S(1)}, bf16[64,512]{1,0:T(8,128)(2,1)S(1)}, u32[]{:S(2)}, u32[]{:S(2)}) %collective-permute-start.1) | collective-permute-done | bytes 65568 | tf_op jit(solution)/shard_map/ppermute | solution.py:232
  63.7 1.7 %collective-permute-done.refs_1_ = bf16[64,512]{1,0:T(8,128)(2,1)S(1)} collective-permute-done((bf16[64,512]{1,0:T(8,128)(2,1)S(1)}, bf16[64,512]{1,0:T(8,128)(2,1)S(1)}, u32[]{:S(2)}, u32[]{:S(2)}) %collective-permute-start) | collective-permute-done | bytes 65568 | tf_op jit(solution)/shard_map/ppermute | solution.py:232
  65.5 5.8 %all-to-all-done.1 = bf16[128,32,128]{2,1,0:T(8,128)(2,1)S(1)} async-done(((bf16[128,32,128]{2,1,0:T(8,128)(2,1)}), bf16[128,32,128]{2,1,0:T(8,128)(2,1)S(1)}, u32[]{:S(2)}, u32[]{:S(2)}) %all-to-all-start.1) | async-done | bytes 1048608 | tf_op jit(solution)/shard_map/all_to_all | solution.py:229
  71.2 0.0 copy-done
  71.2 3.9 %shard_map.86 = bf16[64,512]{1,0:T(8,128)(2,1)} custom-call(bf16[64,512]{1,0:T(8,128)(2,1)S(1)} %get-tuple-element.17.table, bf16[4096,128]{1,0:T(8,128)(2,1)S(1)} %bitcast.14, s32[1,512]{1,0:T(1,128)S(1)} %bitcast.15, f8e4m3fn[8704,512]{1,0:T(32,128)(4,1)} %shard_map.85.counts_hbm, bf16[64,512]{1,0:T(8,128)(2,1)S(1)} %get-tuple-element.26.refs_0_, ...), custom_call_target="tpu_custom_call" | custom-call | flops 570425344 | bytes 10485760 | tf_op jit(solution)/shard_map/pallas_call | solution.py:197
  (3 shorter events, 0.0 us)
Async XLA Ops:
  2.3 10.3 %all-to-all-start = ((bf16[4,64,512]{2,1,0:T(8,128)(2,1)}), bf16[4,64,512]{2,1,0:T(8,128)(2,1)S(1)}, u32[]{:S(2)}, u32[]{:S(2)}) async-start(bf16[4,64,512]{2,1,0:T(8,128)(2,1)} %shard_map.82), calls=%async_computation | async-start | bytes 524288 | tf_op jit(solution)/shard_map/all_to_all | solution.py:213
  15.3 56.0 %all-to-all-start.1 = ((bf16[128,32,128]{2,1,0:T(8,128)(2,1)}), bf16[128,32,128]{2,1,0:T(8,128)(2,1)S(1)}, u32[]{:S(2)}, u32[]{:S(2)}) async-start(bf16[128,32,128]{2,1,0:T(8,128)(2,1)} %bitcast.2), calls=%async_computation.1 | async-start | bytes 2097152 | tf_op jit(solution)/shard_map/all_to_all | solution.py:229
  36.1 23.5 %collective-permute-start.2 = (bf16[64,512]{1,0:T(8,128)(2,1)S(1)}, bf16[64,512]{1,0:T(8,128)(2,1)S(1)}, u32[]{:S(2)}, u32[]{:S(2)}) collective-permute-start(bf16[64,512]{1,0:T(8,128)(2,1)S(1)} %get-tuple-element.23), channel_id=1, source_target_pairs={{0,384},{128,0},{256,128},{384,256},{1,385},{129,1},{257,129},{385... | collective-permute-start | bytes 196616 | tf_op jit(solution)/shard_map/ppermute | solution.py:232
  39.7 24.1 %collective-permute-start.1 = (bf16[64,512]{1,0:T(8,128)(2,1)S(1)}, bf16[64,512]{1,0:T(8,128)(2,1)S(1)}, u32[]{:S(2)}, u32[]{:S(2)}) collective-permute-start(bf16[64,512]{1,0:T(8,128)(2,1)S(1)} %get-tuple-element.24), channel_id=1, source_target_pairs={{0,256},{128,384},{256,0},{384,128},{1,257},{129,385},{257,1},{385... | collective-permute-start | bytes 196616 | tf_op jit(solution)/shard_map/ppermute | solution.py:232
  41.6 29.6 %copy-start = (s32[512]{0:T(512)S(1)}, s32[512]{0:T(512)}, u32[]{:S(2)}) copy-start(s32[512]{0:T(512)} %param.13) | copy-start | bytes 6148
  41.6 23.8 %collective-permute-start = (bf16[64,512]{1,0:T(8,128)(2,1)S(1)}, bf16[64,512]{1,0:T(8,128)(2,1)S(1)}, u32[]{:S(2)}, u32[]{:S(2)}) collective-permute-start(bf16[64,512]{1,0:T(8,128)(2,1)S(1)} %get-tuple-element.25), channel_id=1, source_target_pairs={{0,128},{128,256},{256,384},{384,0},{1,129},{129,257},{257,385},{3... | collective-permute-start | bytes 196616 | tf_op jit(solution)/shard_map/ppermute | solution.py:232

commit v4 on v3

v4 whole, which is shorter than its diff:
```python
import jax
import jax.numpy as jnp
from jax import lax
from jax.experimental import pallas as pl
from jax.experimental.pallas import tpu as pltpu
from jax.sharding import PartitionSpec as P

F32 = jnp.float32
BF16 = jnp.bfloat16
F8 = jnp.float8_e4m3fn
VMEM = pl.BlockSpec(memory_space=pltpu.VMEM)
ANY = pl.BlockSpec(memory_space=pl.ANY)
LIMIT = pltpu.CompilerParams(vmem_limit_bytes=24 * 1024 * 1024)
CAP = 64
PACK, BITS = 6, 5
HALF = CAP // 2


def cost(flops, nbytes):
    return pl.CostEstimate(flops=flops, bytes_accessed=nbytes, transcendentals=0)


def dot(left, right, dims):
    return lax.dot_general(left, right, (dims, ((), ())), preferred_element_type=F32)


def fetch(sources, targets, arrived):
    copies = [pltpu.make_async_copy(*pair, arrived.at[i]) for i, pair in enumerate(zip(sources, targets))]
    for copy in copies:
        copy.start()
    return copies


def product(copies, weight, proj, features):
    copies[0].wait()
    copies[1].wait()
    joined = dot(weight[...], proj[...], ((0,), (1,)))
    high = joined.astype(BF16)
    low = (joined - high.astype(F32)).astype(BF16)
    copies[2].wait()
    return dot(high, features[...], ((1,), (0,))) + dot(low, features[...], ((1,), (0,)))


def scratch_of(arrays):
    return [pltpu.VMEM(array.shape, array.dtype) for array in arrays] + [pltpu.SemaphoreType.DMA((len(arrays),))]


def in_hbm(arrays):
    return [pltpu.with_memory_space_constraint(array, pltpu.HBM) for array in arrays]


def sent_kernel(weight_hbm, proj_hbm, features_hbm, out, weight, proj, features, arrived):
    copies = fetch((weight_hbm, proj_hbm, features_hbm), (weight, proj, features), arrived)
    out[...] = product(copies, weight, proj, features).astype(BF16).reshape(out.shape)


def sent_partials(weight, proj, features, columns):
    width, nodes = weight.shape[1], features.shape[1]
    arrays = (weight, proj, features)
    return pl.pallas_call(
        sent_kernel,
        out_shape=jax.ShapeDtypeStruct((columns, width // columns, nodes), BF16),
        in_specs=[ANY] * 3,
        out_specs=VMEM,
        scratch_shapes=scratch_of(arrays),
        compiler_params=LIMIT,
        cost_estimate=cost(2 * width * nodes * 640, 1 << 20),
    )(*in_hbm(arrays))


def side_kernel(*refs):
    sources, (kept, given, wanted), targets = refs[:5], refs[5:8], refs[8:13]
    arrived, wide, spread, limits = refs[13:]
    weight, proj, features, rows, live = targets
    copies = fetch(sources, targets, arrived)
    wide[...] = product(copies, weight, proj, features)
    depth = kept.shape[1]
    me = lax.axis_index("cols")
    pair, odd = me // 2, lax.rem(me, 2)
    for i in range(2):
        first = 2 * (pair if i == 0 else 1 - pair)
        start = pl.multiple_of((first + odd) * depth, depth)
        kept[i] = wide[pl.ds(start, depth), :]
        start = pl.multiple_of((first + 1 - odd) * depth, depth)
        given[i] = wide[pl.ds(start, depth), :].astype(BF16)
    copies[3].wait()
    copies[4].wait()
    lines = spread.shape[0]
    for i in range(lines):
        spread[pl.ds(i, 1), :] = rows[:, pl.ds(i * 128, 128)]
    limits[...] = jnp.broadcast_to(live[...], limits.shape).astype(F32).T
    lane = lax.broadcasted_iota(jnp.int32, (lines // 2, 128), 1)
    halves = []
    for k in range(2):
        low = limits[pl.ds(2 * k, lines // 2, stride=4), :]
        high = limits[pl.ds(2 * k + 1, lines // 2, stride=4), :]
        alive = (lane & (CAP - 1)).astype(F32) < jnp.where(lane < CAP, low, high)
        halves.append(jnp.where(alive, spread[pl.ds(k, lines // 2, stride=2), :], -1))
    even, odd = halves
    for h in range(2):
        parts = [pltpu.roll(source, (128 + to - HALF * h) % 128, 1) for source, to in ((even, 0), (even, -32), (odd, 64), (odd, 32))]
        wanted[h] = jnp.where(
            lane < 64, jnp.where(lane < 32, parts[0], parts[1]), jnp.where(lane < 96, parts[2], parts[3])
        )


def side(weight, proj, features, send_rows, send_count, columns):
    width, nodes = weight.shape[1], features.shape[1]
    depth = width // columns
    lines = send_rows.shape[1] // 128
    arrays = (weight, proj, features, send_rows, send_count)
    return pl.pallas_call(
        side_kernel,
        out_shape=(
            jax.ShapeDtypeStruct((2, depth, nodes), F32),
            jax.ShapeDtypeStruct((2, depth, nodes), BF16),
            jax.ShapeDtypeStruct((2, lines // 2, 128), jnp.int32),
        ),
        in_specs=[ANY] * 5,
        out_specs=(VMEM,) * 3,
        scratch_shapes=scratch_of(arrays)
        + [
            pltpu.VMEM((width, nodes), F32),
            pltpu.VMEM((lines, 128), jnp.int32),
            pltpu.VMEM((send_count.shape[1], 128), F32),
        ],
        compiler_params=LIMIT,
        cost_estimate=cost(2 * width * nodes * 640, 1 << 20),
    )(*in_hbm(arrays))


def select_kernel(sent, wanted, rows_hbm, table, rows, left):
    width, nodes = table.shape
    total = sent[0].astype(F32)
    for c in range(1, sent.shape[0]):
        total = total + sent[c].astype(F32)
    table[...] = total.astype(BF16)
    stacked = jnp.concatenate([table[:, :256], table[:, 256:]], axis=0)
    step = 256
    iota = lax.broadcasted_iota(jnp.int32, (256, step), 0).astype(F32).astype(BF16)
    copies = []
    for start in range(0, rows.shape[0], step):
        halves = []
        for h in range(2):
            lines = [wanted[h, pl.ds((start + at) // 128, 1), :] for at in range(0, step, 128)]
            codes = jnp.concatenate(lines, axis=1)
            low = jnp.where(codes >= 0, codes & 255, -1).astype(F32)
            low = jnp.broadcast_to(low, (16, step)).astype(BF16)
            low = jnp.broadcast_to(low[None], (16, 16, step)).reshape(256, step)
            onehot = jnp.where(iota == low, jnp.ones((), BF16), jnp.zeros((), BF16))
            both = dot(stacked, onehot, ((1,), (0,)))
            picked = jnp.where(codes >= 256, both[width:], both[:width])
            halves.append(picked)
        at = pl.ds(start, step)
        rows[at, :] = jnp.concatenate(halves, axis=0).T.astype(BF16)
        copies.append(pltpu.make_async_copy(rows.at[at], rows_hbm.at[at], left.at[len(copies)]))
        copies[-1].start()
    for copy in copies:
        copy.wait()


def select(sent, wanted):
    width, nodes = sent.shape[1], sent.shape[2]
    columns = wanted.shape[1] * 128
    return pl.pallas_call(
        select_kernel,
        out_shape=(
            pltpu.HBM((columns, 2 * width), BF16),
            jax.ShapeDtypeStruct((width, nodes), BF16),
        ),
        in_specs=[VMEM] * 2,
        out_specs=(ANY, VMEM),
        scratch_shapes=[pltpu.VMEM((columns, 2 * width), BF16), pltpu.SemaphoreType.DMA((columns // 256,))],
        compiler_params=LIMIT,
        cost_estimate=cost(4 * width * nodes * columns, 1 << 20),
    )(sent, wanted)


def count_kernel(neighbors_hbm, degree_hbm, near, far, neighbors, degree, arrived, codes, spread, stage, left):
    slots, nodes = codes.shape
    for copy in fetch((neighbors_hbm, degree_hbm), (neighbors, degree), arrived):
        copy.wait()
    rows = near.shape[0] + far.shape[0]
    code = neighbors[...] - nodes
    part, slot = code >> 6, code & (CAP - 1)
    remote = nodes + (slot >> 5) * ((rows - nodes) // 2) + part * HALF + (slot & (HALF - 1))
    used = lax.broadcasted_iota(jnp.int32, (slots, nodes), 0) < degree[...]
    codes[...] = jnp.where(used, jnp.where(code >= 0, remote, code + nodes), -1)
    block, strip = stage.shape[1] // PACK, 32
    span = PACK * block
    iota = lax.broadcasted_iota(jnp.int32, (strip, nodes), 0)

    def group(i, write):
        code = codes[...] - i * span
        inside = jnp.logical_and(code >= 0, code < span)
        spread[0] = jnp.where(inside, code & (block - 1), -1)
        spread[1] = jnp.where(inside, 1 << ((code >> 7) * BITS), 0)
        for low in range(0, block, strip):
            places = iota + low
            total = jnp.zeros((strip, nodes), jnp.int32)
            for k in range(slots):
                total = total + jnp.where(places == spread[0, k : k + 1, :], spread[1, k : k + 1, :], 0)
            for j in range(PACK):
                part = (total >> (j * BITS)) & (2**BITS - 1)
                write(j * block + low, part.astype(F32).astype(F8))

    def near_step(i, carry):
        def write(low, part):
            near[pl.ds(pl.multiple_of(i * span + low, strip), strip), :] = part

        group(i, write)
        return carry

    def move(i, size, turn):
        return pltpu.make_async_copy(
            stage.at[turn, pl.ds(0, size)], far.at[pl.ds(i * span, size)], left.at[turn]
        )

    def far_group(i, turn):
        def write(low, part):
            stage[turn, pl.ds(low, strip), :] = part

        group(near.shape[0] // span + i, write)

    def far_step(i, carry):
        turn = lax.rem(i, 2)

        @pl.when(i >= 2)
        def _():
            move(i - 2, span, turn).wait()

        far_group(i, turn)
        move(i, span, turn).start()
        return carry

    lax.fori_loop(0, near.shape[0] // span, near_step, 0)
    last = pl.cdiv(far.shape[0], span) - 1
    size = far.shape[0] - last * span
    lax.fori_loop(0, last, far_step, 0)
    move(last - 2, span, last % 2).wait()
    far_group(last, last % 2)
    move(last, size, last % 2).start()
    move(last - 1, span, (last - 1) % 2).wait()
    move(last, size, last % 2).wait()


def count(neighbors, degree, rows):
    slots, nodes = neighbors.shape
    near = PACK * 128 * 4
    arrays = (neighbors, degree)
    return pl.pallas_call(
        count_kernel,
        out_shape=(jax.ShapeDtypeStruct((near, nodes), F8), pltpu.HBM((rows - near, nodes), F8)),
        in_specs=[ANY] * 2,
        out_specs=(VMEM, ANY),
        scratch_shapes=scratch_of(arrays)
        + [
            pltpu.VMEM((slots, nodes), jnp.int32),
            pltpu.VMEM((2, slots, nodes), jnp.int32),
            pltpu.VMEM((2, PACK * 128, nodes), F8),
            pltpu.SemaphoreType.DMA((2,)),
        ],
        compiler_params=LIMIT,
        cost_estimate=cost(9 * 10**9, 20 << 20),
    )(*in_hbm(arrays))


def combine_kernel(table, rows, degree, first, counts_hbm, kept, near, far, out, second, arrived):
    width, nodes = table.shape
    depth = rows.shape[0]
    chunk = 512
    copies = []
    for i in range(second.shape[0] // chunk):
        at = pl.ds(i * chunk, chunk)
        copies.append(pltpu.make_async_copy(counts_hbm.at[at], second.at[at], arrived.at[i]))
        copies[i].start()
    total = jnp.zeros((width, nodes), F32)
    for start in range(0, nodes + 2 * depth, chunk):
        if start < nodes:
            left = table[:, start : start + chunk]
        else:
            h, low = divmod(start - nodes, depth)
            left = rows[low : low + chunk, h * width : (h + 1) * width].astype(F32).T.astype(BF16)
        if start < first.shape[0]:
            counts = first[pl.ds(start, chunk), :]
        else:
            at = start - first.shape[0]
            copies[at // chunk].wait()
            counts = second[pl.ds(at, chunk), :]
        total = total + dot(left, counts.astype(BF16), ((1,), (0,)))
    own = kept[0] + near[0].astype(F32) + far[...].astype(F32)
    result = own + total / degree[...].astype(F32)
    out[...] = jnp.maximum(result, 0.0).astype(BF16)


def combine(table, rows, degree, counts, kept, near, far):
    width, nodes = table.shape
    first, second = counts
    return pl.pallas_call(
        combine_kernel,
        out_shape=jax.ShapeDtypeStruct((width, nodes), BF16),
        in_specs=[VMEM] * 4 + [ANY] + [VMEM] * 3,
        out_specs=VMEM,
        scratch_shapes=[pltpu.VMEM(second.shape, F8), pltpu.SemaphoreType.DMA((second.shape[0] // 512,))],
        compiler_params=LIMIT,
        cost_estimate=cost(2 * width * nodes * 8704, 10 << 20),
    )(table, rows, degree, first, *in_hbm([second]), kept, near, far)


def local(features, proj_in, self_weight, neigh_weight, neighbors, degree, send_rows, send_count):
    columns = lax.axis_size("cols")
    degree = degree[None, :]
    sent = sent_partials(neigh_weight, proj_in, features, columns)
    sent, send_rows = lax.optimization_barrier((sent, send_rows))
    sent = lax.all_to_all(sent, "cols", 0, 0, tiled=True)

    kept, given, wanted = side(self_weight, proj_in, features, send_rows, send_count, columns)
    near = lax.ppermute(given, "cols", [(c, c ^ 1) for c in range(columns)])

    chosen, table = select(sent, wanted)
    chosen, near = lax.optimization_barrier((chosen, near))
    far = (kept[1] + near[1].astype(F32)).astype(BF16)
    chosen, neighbors, far = lax.optimization_barrier((chosen, neighbors, far))
    rows = lax.all_to_all(chosen.reshape(-1, HALF, chosen.shape[1]), "dom", 0, 0, tiled=True)
    far = lax.ppermute(far, "cols", [(c, c ^ 2) for c in range(columns)])
    counts = count(neighbors, degree, neighbors.shape[1] + 2 * chosen.shape[0])
    return combine(table, rows.reshape(chosen.shape), degree, counts, kept, near, far)


def solution(mesh):
    return jax.shard_map(
        local,
        mesh=mesh,
        in_specs=(
            P("cols", "dom"),
            P("cols", None),
            P(),
            P(),
            P(None, "dom"),
            P("dom"),
            P("dom", None),
            P("dom", None),
        ),
        out_specs=P("cols", "dom"),
        check_vma=False,
    )
```

time: 75.7 us -> 74.9 us (0.989)
  the two profiles are of different devices: /device:TPU:9 before, /device:TPU:17 now
where the time goes in v4:
time: 74.9 us; the launch traced here: 74.4 us
  starting transfers between devices  30.5 us (41%)
  waiting for transfers between devices  25 us (33%)
  Pallas kernels  18.8 us (25%)
    all_to_all x1, starting transfers between devices, local(): lax.all_to_all(chosen.reshape(-1, HALF, chosen.shape[1]), 'dom', 0, 0, ti...  19.3 us
    ppermute x1, waiting for transfers between devices, local(): far = lax.ppermute(far, 'cols', [(c, c ^ 2) for c in range(columns)])  11.4 us
    all_to_all x1, waiting for transfers between devices, local(): lax.all_to_all(chosen.reshape(-1, HALF, chosen.shape[1]), 'dom', 0, 0, ti...  11.3 us
    pallas_call x1, Pallas kernels, count(): pl.pallas_call(count_kernel, out_shape=(jax.ShapeDtypeStruct((near, nodes...  9.36 us
    all_to_all x1, starting transfers between devices, local(): sent = lax.all_to_all(sent, 'cols', 0, 0, tiled=True)  4.66 us
    pallas_call x1, Pallas kernels, combine(): pl.pallas_call(combine_kernel, out_shape=jax.ShapeDtypeStruct((width, nod...  3.74 us
    ppermute x1, starting transfers between devices, local(): far = lax.ppermute(far, 'cols', [(c, c ^ 2) for c in range(columns)])  3.46 us
    ppermute x1, starting transfers between devices, local(): near = lax.ppermute(given, 'cols', [(c, c ^ 1) for c in range(columns)])  3.09 us
  transfers between devices with their start and end apart: 4, of which 3 were waited for; matrix products, arithmetic and copies ran while one was open for 0% of the time, Pallas kernels for 17%

profile of v4, /device:TPU:17, one launch (start us, length us, event | category | flops | bytes accessed | tf_op | source)
XLA Modules:
  0.0 74.4 jit_solution(3528539110163392746)
XLA Ops:
  0.0 2.3 %shard_map.82 = bf16[4,64,512]{2,1,0:T(8,128)(2,1)} custom-call(bf16[256,256]{1,0:T(8,128)(2,1)} %weight_hbm.1, bf16[192,256]{1,0:T(8,128)(2,1)} %refs_1_.1, bf16[192,512]{1,0:T(8,128)(2,1)} %refs_2_.1), custom_call_target="tpu_custom_call" | custom-call | flops 167772160 | bytes 1048576 | tf_op jit(solution)/shard_map/pallas_call | solution.py:60
  2.3 4.7 %all-to-all-start = ((bf16[4,64,512]{2,1,0:T(8,128)(2,1)}), bf16[4,64,512]{2,1,0:T(8,128)(2,1)S(1)}, u32[]{:S(2)}, u32[]{:S(2)}) async-start(bf16[4,64,512]{2,1,0:T(8,128)(2,1)} %shard_map.82), calls=%async_computation | async-start | bytes 524288 | tf_op jit(solution)/shard_map/all_to_all | solution.py:315
  6.9 1.8 %shard_map.83 = (f32[2,64,512]{2,1,0:T(8,128)S(1)}, bf16[2,64,512]{2,1,0:T(8,128)(2,1)S(1)}, s32[2,32,128]{2,1,0:T(8,128)S(1)}) custom-call(bf16[256,256]{1,0:T(8,128)(2,1)} %refs_0_.1, bf16[192,256]{1,0:T(8,128)(2,1)} %refs_1_.1, bf16[192,512]{1,0:T(8,128)(2,1)} %refs_2_.1, s32[1,8192]{1,0:T(1,128)} %refs_3_, s32[1,128]{1,0:T(1,128)} %refs_4_.1), custom_call_target="tpu_custom_call" | custom-call | flops 167772160 | bytes 1048576 | tf_op jit(solution)/shard_map/pallas_call | solution.py:112
  8.7 3.1 %collective-permute-start = (bf16[2,64,512]{2,1,0:T(8,128)(2,1)S(1)}, bf16[2,64,512]{2,1,0:T(8,128)(2,1)S(1)}, u32[]{:S(2)}, u32[]{:S(2)}) collective-permute-start(bf16[2,64,512]{2,1,0:T(8,128)(2,1)S(1)} %get-tuple-element.24), channel_id=1, source_target_pairs={{0,128},{128,0},{256,384},{384,256},{1,129},{129,1},{257,385},{385... | collective-permute-start | bytes 393224 | tf_op jit(solution)/shard_map/ppermute | solution.py:318
  11.8 0.0 all-to-all-done.sent
  11.8 1.7 %shard_map.84 = (bf16[4096,128]{1,0:T(8,128)(2,1)}, bf16[64,512]{1,0:T(8,128)(2,1)S(1)}) custom-call(bf16[4,64,512]{2,1,0:T(8,128)(2,1)S(1)} %all-to-all-done.sent, s32[2,32,128]{2,1,0:T(8,128)S(1)} %get-tuple-element.21.wanted), custom_call_target="tpu_custom_call" | custom-call | flops 536870912 | bytes 1048576 | tf_op jit(solution)/shard_map/pallas_call | solution.py:165
  13.5 2.3 %collective-permute-done.near = bf16[2,64,512]{2,1,0:T(8,128)(2,1)S(1)} collective-permute-done((bf16[2,64,512]{2,1,0:T(8,128)(2,1)S(1)}, bf16[2,64,512]{2,1,0:T(8,128)(2,1)S(1)}, u32[]{:S(2)}, u32[]{:S(2)}) %collective-permute-start) | collective-permute-done | bytes 131104 | tf_op jit(solution)/shard_map/ppermute | solution.py:318
  15.9 19.3 %all-to-all-start.1 = ((bf16[128,32,128]{2,1,0:T(8,128)(2,1)}), bf16[128,32,128]{2,1,0:T(8,128)(2,1)S(1)}, u32[]{:S(2)}, u32[]{:S(2)}) async-start(bf16[128,32,128]{2,1,0:T(8,128)(2,1)} %bitcast.8), calls=%async_computation.1 | async-start | bytes 2097152 | tf_op jit(solution)/shard_map/all_to_all | solution.py:324
  35.2 3.5 %collective-permute-start.1 = (bf16[64,512]{1,0:T(8,128)(2,1)S(1)}, bf16[64,512]{1,0:T(8,128)(2,1)S(1)}, u32[]{:S(2)}, u32[]{:S(2)}) collective-permute-start(bf16[64,512]{1,0:T(8,128)(2,1)S(1)} %fusion), channel_id=1, source_target_pairs={{0,256},{128,384},{256,0},{384,128},{1,257},{129,385},{257,1},{385... | collective-permute-start | bytes 196616 | tf_op jit(solution)/shard_map/ppermute | solution.py:325
  38.6 0.0 copy-start
  38.7 9.4 %shard_map.85 = (f8e4m3fn[3072,512]{1,0:T(32,128)(4,1)S(1)}, f8e4m3fn[5632,512]{1,0:T(32,128)(4,1)}) custom-call(s32[16,512]{1,0:T(8,128)} %neighbors_hbm, s32[1,512]{1,0:T(1,128)} %bitcast.6), custom_call_target="tpu_custom_call" | custom-call | flops 8999999488 | bytes 20971520 | tf_op jit(solution)/shard_map/pallas_call | solution.py:251
  48.0 11.4 %collective-permute-done.1.far = bf16[64,512]{1,0:T(8,128)(2,1)S(1)} collective-permute-done((bf16[64,512]{1,0:T(8,128)(2,1)S(1)}, bf16[64,512]{1,0:T(8,128)(2,1)S(1)}, u32[]{:S(2)}, u32[]{:S(2)}) %collective-permute-start.1) | collective-permute-done | bytes 65568 | tf_op jit(solution)/shard_map/ppermute | solution.py:325
  59.4 11.3 %all-to-all-done.1 = bf16[128,32,128]{2,1,0:T(8,128)(2,1)S(1)} async-done(((bf16[128,32,128]{2,1,0:T(8,128)(2,1)}), bf16[128,32,128]{2,1,0:T(8,128)(2,1)S(1)}, u32[]{:S(2)}, u32[]{:S(2)}) %all-to-all-start.1) | async-done | bytes 1048608 | tf_op jit(solution)/shard_map/all_to_all | solution.py:324
  70.7 0.0 copy-done
  70.7 3.7 %shard_map.86 = bf16[64,512]{1,0:T(8,128)(2,1)} custom-call(bf16[64,512]{1,0:T(8,128)(2,1)S(1)} %get-tuple-element.22.table, bf16[4096,128]{1,0:T(8,128)(2,1)S(1)} %bitcast.5, s32[1,512]{1,0:T(1,128)S(1)} %bitcast.7, f8e4m3fn[3072,512]{1,0:T(32,128)(4,1)S(1)} %get-tuple-element.30.first, f8e4m3fn[5632,512]{1,0:T(32,128)(4,1)} %get-tuple-element.31.counts_hbm, ...), custom_call_target="tpu_custom_call" | custom-call | flops 570425344 | bytes 10485760 | tf_op jit(solution)/shard_map/pallas_call | solution.py:299
  (1 shorter events, 0.0 us)
Async XLA Ops:
  2.3 9.6 %all-to-all-start = ((bf16[4,64,512]{2,1,0:T(8,128)(2,1)}), bf16[4,64,512]{2,1,0:T(8,128)(2,1)S(1)}, u32[]{:S(2)}, u32[]{:S(2)}) async-start(bf16[4,64,512]{2,1,0:T(8,128)(2,1)} %shard_map.82), calls=%async_computation | async-start | bytes 524288 | tf_op jit(solution)/shard_map/all_to_all | solution.py:315
  8.7 7.1 %collective-permute-start = (bf16[2,64,512]{2,1,0:T(8,128)(2,1)S(1)}, bf16[2,64,512]{2,1,0:T(8,128)(2,1)S(1)}, u32[]{:S(2)}, u32[]{:S(2)}) collective-permute-start(bf16[2,64,512]{2,1,0:T(8,128)(2,1)S(1)} %get-tuple-element.24), channel_id=1, source_target_pairs={{0,128},{128,0},{256,384},{384,256},{1,129},{129,1},{257,385},{385... | collective-permute-start | bytes 393224 | tf_op jit(solution)/shard_map/ppermute | solution.py:318
  15.9 54.8 %all-to-all-start.1 = ((bf16[128,32,128]{2,1,0:T(8,128)(2,1)}), bf16[128,32,128]{2,1,0:T(8,128)(2,1)S(1)}, u32[]{:S(2)}, u32[]{:S(2)}) async-start(bf16[128,32,128]{2,1,0:T(8,128)(2,1)} %bitcast.8), calls=%async_computation.1 | async-start | bytes 2097152 | tf_op jit(solution)/shard_map/all_to_all | solution.py:324
  35.2 24.2 %collective-permute-start.1 = (bf16[64,512]{1,0:T(8,128)(2,1)S(1)}, bf16[64,512]{1,0:T(8,128)(2,1)S(1)}, u32[]{:S(2)}, u32[]{:S(2)}) collective-permute-start(bf16[64,512]{1,0:T(8,128)(2,1)S(1)} %fusion), channel_id=1, source_target_pairs={{0,256},{128,384},{256,0},{384,128},{1,257},{129,385},{257,1},{385... | collective-permute-start | bytes 196616 | tf_op jit(solution)/shard_map/ppermute | solution.py:325
  38.6 32.0 %copy-start = (s32[512]{0:T(512)S(1)}, s32[512]{0:T(512)}, u32[]{:S(2)}) copy-start(s32[512]{0:T(512)} %param.13) | copy-start | bytes 6148

commit v5 on v4

--- a/solution.py
+++ b/solution.py
@@ -274,13 +274,16 @@
         at = pl.ds(i * chunk, chunk)
         copies.append(pltpu.make_async_copy(counts_hbm.at[at], second.at[at], arrived.at[i]))
         copies[i].start()
+    turned = []
     total = jnp.zeros((width, nodes), F32)
     for start in range(0, nodes + 2 * depth, chunk):
         if start < nodes:
             left = table[:, start : start + chunk]
         else:
             h, low = divmod(start - nodes, depth)
-            left = rows[low : low + chunk, h * width : (h + 1) * width].astype(F32).T.astype(BF16)
+            if h == 0:
+                turned.append(rows[low : low + chunk, :].astype(F32).T.astype(BF16))
+            left = turned[low // chunk][h * width : (h + 1) * width]
         if start < first.shape[0]:
             counts = first[pl.ds(start, chunk), :]
         else:

time: 74.9 us -> 74.1 us (0.989)
  no operation moved by 1% of the time
where the time goes in v5:
time: 74.1 us; the launch traced here: 73.7 us
  starting transfers between devices  30.5 us (41%)
  waiting for transfers between devices  25 us (34%)
  Pallas kernels  18.1 us (24%)
    all_to_all x1, starting transfers between devices, local(): lax.all_to_all(chosen.reshape(-1, HALF, chosen.shape[1]), 'dom', 0, 0, ti...  19.3 us
    ppermute x1, waiting for transfers between devices, local(): far = lax.ppermute(far, 'cols', [(c, c ^ 2) for c in range(columns)])  11.4 us
    all_to_all x1, waiting for transfers between devices, local(): lax.all_to_all(chosen.reshape(-1, HALF, chosen.shape[1]), 'dom', 0, 0, ti...  11.3 us
    pallas_call x1, Pallas kernels, count(): pl.pallas_call(count_kernel, out_shape=(jax.ShapeDtypeStruct((near, nodes...  9.36 us
    all_to_all x1, starting transfers between devices, local(): sent = lax.all_to_all(sent, 'cols', 0, 0, tiled=True)  4.66 us
    ppermute x1, starting transfers between devices, local(): far = lax.ppermute(far, 'cols', [(c, c ^ 2) for c in range(columns)])  3.46 us
    ppermute x1, starting transfers between devices, local(): near = lax.ppermute(given, 'cols', [(c, c ^ 1) for c in range(columns)])  3.09 us
    pallas_call x1, Pallas kernels, combine(): pl.pallas_call(combine_kernel, out_shape=jax.ShapeDtypeStruct((width, nod...  3.02 us
  transfers between devices with their start and end apart: 4, of which 3 were waited for; matrix products, arithmetic and copies ran while one was open for 0% of the time, Pallas kernels for 17%

profile of v5, /device:TPU:17, one launch (start us, length us, event | category | flops | bytes accessed | tf_op | source)
XLA Modules:
  0.0 73.7 jit_solution(5942154909946194062)
XLA Ops:
  0.0 2.3 %shard_map.82 = bf16[4,64,512]{2,1,0:T(8,128)(2,1)} custom-call(bf16[256,256]{1,0:T(8,128)(2,1)} %weight_hbm.1, bf16[192,256]{1,0:T(8,128)(2,1)} %refs_1_.1, bf16[192,512]{1,0:T(8,128)(2,1)} %refs_2_.1), custom_call_target="tpu_custom_call" | custom-call | flops 167772160 | bytes 1048576 | tf_op jit(solution)/shard_map/pallas_call | solution.py:60
  2.3 4.7 %all-to-all-start = ((bf16[4,64,512]{2,1,0:T(8,128)(2,1)}), bf16[4,64,512]{2,1,0:T(8,128)(2,1)S(1)}, u32[]{:S(2)}, u32[]{:S(2)}) async-start(bf16[4,64,512]{2,1,0:T(8,128)(2,1)} %shard_map.82), calls=%async_computation | async-start | bytes 524288 | tf_op jit(solution)/shard_map/all_to_all | solution.py:318
  6.9 1.8 %shard_map.83 = (f32[2,64,512]{2,1,0:T(8,128)S(1)}, bf16[2,64,512]{2,1,0:T(8,128)(2,1)S(1)}, s32[2,32,128]{2,1,0:T(8,128)S(1)}) custom-call(bf16[256,256]{1,0:T(8,128)(2,1)} %refs_0_.1, bf16[192,256]{1,0:T(8,128)(2,1)} %refs_1_.1, bf16[192,512]{1,0:T(8,128)(2,1)} %refs_2_.1, s32[1,8192]{1,0:T(1,128)} %refs_3_, s32[1,128]{1,0:T(1,128)} %refs_4_.1), custom_call_target="tpu_custom_call" | custom-call | flops 167772160 | bytes 1048576 | tf_op jit(solution)/shard_map/pallas_call | solution.py:112
  8.7 3.1 %collective-permute-start = (bf16[2,64,512]{2,1,0:T(8,128)(2,1)S(1)}, bf16[2,64,512]{2,1,0:T(8,128)(2,1)S(1)}, u32[]{:S(2)}, u32[]{:S(2)}) collective-permute-start(bf16[2,64,512]{2,1,0:T(8,128)(2,1)S(1)} %get-tuple-element.24), channel_id=1, source_target_pairs={{0,128},{128,0},{256,384},{384,256},{1,129},{129,1},{257,385},{385... | collective-permute-start | bytes 393224 | tf_op jit(solution)/shard_map/ppermute | solution.py:321
  11.8 0.0 all-to-all-done.sent
  11.8 1.7 %shard_map.84 = (bf16[4096,128]{1,0:T(8,128)(2,1)}, bf16[64,512]{1,0:T(8,128)(2,1)S(1)}) custom-call(bf16[4,64,512]{2,1,0:T(8,128)(2,1)S(1)} %all-to-all-done.sent, s32[2,32,128]{2,1,0:T(8,128)S(1)} %get-tuple-element.21.wanted), custom_call_target="tpu_custom_call" | custom-call | flops 536870912 | bytes 1048576 | tf_op jit(solution)/shard_map/pallas_call | solution.py:165
  13.5 2.3 %collective-permute-done.near = bf16[2,64,512]{2,1,0:T(8,128)(2,1)S(1)} collective-permute-done((bf16[2,64,512]{2,1,0:T(8,128)(2,1)S(1)}, bf16[2,64,512]{2,1,0:T(8,128)(2,1)S(1)}, u32[]{:S(2)}, u32[]{:S(2)}) %collective-permute-start) | collective-permute-done | bytes 131104 | tf_op jit(solution)/shard_map/ppermute | solution.py:321
  15.9 19.3 %all-to-all-start.1 = ((bf16[128,32,128]{2,1,0:T(8,128)(2,1)}), bf16[128,32,128]{2,1,0:T(8,128)(2,1)S(1)}, u32[]{:S(2)}, u32[]{:S(2)}) async-start(bf16[128,32,128]{2,1,0:T(8,128)(2,1)} %bitcast.8), calls=%async_computation.1 | async-start | bytes 2097152 | tf_op jit(solution)/shard_map/all_to_all | solution.py:327
  35.2 3.5 %collective-permute-start.1 = (bf16[64,512]{1,0:T(8,128)(2,1)S(1)}, bf16[64,512]{1,0:T(8,128)(2,1)S(1)}, u32[]{:S(2)}, u32[]{:S(2)}) collective-permute-start(bf16[64,512]{1,0:T(8,128)(2,1)S(1)} %fusion), channel_id=1, source_target_pairs={{0,256},{128,384},{256,0},{384,128},{1,257},{129,385},{257,1},{385... | collective-permute-start | bytes 196616 | tf_op jit(solution)/shard_map/ppermute | solution.py:328
  38.6 0.0 copy-start
  38.7 9.4 %shard_map.85 = (f8e4m3fn[3072,512]{1,0:T(32,128)(4,1)S(1)}, f8e4m3fn[5632,512]{1,0:T(32,128)(4,1)}) custom-call(s32[16,512]{1,0:T(8,128)} %neighbors_hbm, s32[1,512]{1,0:T(1,128)} %bitcast.6), custom_call_target="tpu_custom_call" | custom-call | flops 8999999488 | bytes 20971520 | tf_op jit(solution)/shard_map/pallas_call | solution.py:251
  48.0 11.4 %collective-permute-done.1.far = bf16[64,512]{1,0:T(8,128)(2,1)S(1)} collective-permute-done((bf16[64,512]{1,0:T(8,128)(2,1)S(1)}, bf16[64,512]{1,0:T(8,128)(2,1)S(1)}, u32[]{:S(2)}, u32[]{:S(2)}) %collective-permute-start.1) | collective-permute-done | bytes 65568 | tf_op jit(solution)/shard_map/ppermute | solution.py:328
  59.4 11.3 %all-to-all-done.1 = bf16[128,32,128]{2,1,0:T(8,128)(2,1)S(1)} async-done(((bf16[128,32,128]{2,1,0:T(8,128)(2,1)}), bf16[128,32,128]{2,1,0:T(8,128)(2,1)S(1)}, u32[]{:S(2)}, u32[]{:S(2)}) %all-to-all-start.1) | async-done | bytes 1048608 | tf_op jit(solution)/shard_map/all_to_all | solution.py:327
  70.7 0.0 copy-done
  70.7 3.0 %shard_map.86 = bf16[64,512]{1,0:T(8,128)(2,1)} custom-call(bf16[64,512]{1,0:T(8,128)(2,1)S(1)} %get-tuple-element.22.table, bf16[4096,128]{1,0:T(8,128)(2,1)S(1)} %bitcast.5, s32[1,512]{1,0:T(1,128)S(1)} %bitcast.7, f8e4m3fn[3072,512]{1,0:T(32,128)(4,1)S(1)} %get-tuple-element.30.first, f8e4m3fn[5632,512]{1,0:T(32,128)(4,1)} %get-tuple-element.31.counts_hbm, ...), custom_call_target="tpu_custom_call" | custom-call | flops 570425344 | bytes 10485760 | tf_op jit(solution)/shard_map/pallas_call | solution.py:302
  (1 shorter events, 0.0 us)
Async XLA Ops:
  2.3 9.6 %all-to-all-start = ((bf16[4,64,512]{2,1,0:T(8,128)(2,1)}), bf16[4,64,512]{2,1,0:T(8,128)(2,1)S(1)}, u32[]{:S(2)}, u32[]{:S(2)}) async-start(bf16[4,64,512]{2,1,0:T(8,128)(2,1)} %shard_map.82), calls=%async_computation | async-start | bytes 524288 | tf_op jit(solution)/shard_map/all_to_all | solution.py:318
  8.7 7.1 %collective-permute-start = (bf16[2,64,512]{2,1,0:T(8,128)(2,1)S(1)}, bf16[2,64,512]{2,1,0:T(8,128)(2,1)S(1)}, u32[]{:S(2)}, u32[]{:S(2)}) collective-permute-start(bf16[2,64,512]{2,1,0:T(8,128)(2,1)S(1)} %get-tuple-element.24), channel_id=1, source_target_pairs={{0,128},{128,0},{256,384},{384,256},{1,129},{129,1},{257,385},{385... | collective-permute-start | bytes 393224 | tf_op jit(solution)/shard_map/ppermute | solution.py:321
  15.9 54.8 %all-to-all-start.1 = ((bf16[128,32,128]{2,1,0:T(8,128)(2,1)}), bf16[128,32,128]{2,1,0:T(8,128)(2,1)S(1)}, u32[]{:S(2)}, u32[]{:S(2)}) async-start(bf16[128,32,128]{2,1,0:T(8,128)(2,1)} %bitcast.8), calls=%async_computation.1 | async-start | bytes 2097152 | tf_op jit(solution)/shard_map/all_to_all | solution.py:327
  35.2 24.2 %collective-permute-start.1 = (bf16[64,512]{1,0:T(8,128)(2,1)S(1)}, bf16[64,512]{1,0:T(8,128)(2,1)S(1)}, u32[]{:S(2)}, u32[]{:S(2)}) collective-permute-start(bf16[64,512]{1,0:T(8,128)(2,1)S(1)} %fusion), channel_id=1, source_target_pairs={{0,256},{128,384},{256,0},{384,128},{1,257},{129,385},{257,1},{385... | collective-permute-start | bytes 196616 | tf_op jit(solution)/shard_map/ppermute | solution.py:328
  38.6 32.0 %copy-start = (s32[512]{0:T(512)S(1)}, s32[512]{0:T(512)}, u32[]{:S(2)}) copy-start(s32[512]{0:T(512)} %param.13) | copy-start | bytes 6148

commit v6 on v5

--- a/solution.py
+++ b/solution.py
@@ -290,7 +290,7 @@
             at = start - first.shape[0]
             copies[at // chunk].wait()
             counts = second[pl.ds(at, chunk), :]
-        total = total + dot(left, counts.astype(BF16), ((1,), (0,)))
+        total = total + dot(left, counts, ((1,), (0,)))
     own = kept[0] + near[0].astype(F32) + far[...].astype(F32)
     result = own + total / degree[...].astype(F32)
     out[...] = jnp.maximum(result, 0.0).astype(BF16)

time: 74.1 us -> 73.8 us (level)
  no operation moved by 1% of the time
where the time goes in v6:
time: 73.8 us; the launch traced here: 73.4 us
  starting transfers between devices  30.5 us (41%)
  waiting for transfers between devices  25 us (34%)
  Pallas kernels  17.8 us (24%)
    all_to_all x1, starting transfers between devices, local(): lax.all_to_all(chosen.reshape(-1, HALF, chosen.shape[1]), 'dom', 0, 0, ti...  19.3 us
    ppermute x1, waiting for transfers between devices, local(): far = lax.ppermute(far, 'cols', [(c, c ^ 2) for c in range(columns)])  11.4 us
    all_to_all x1, waiting for transfers between devices, local(): lax.all_to_all(chosen.reshape(-1, HALF, chosen.shape[1]), 'dom', 0, 0, ti...  11.3 us
    pallas_call x1, Pallas kernels, count(): pl.pallas_call(count_kernel, out_shape=(jax.ShapeDtypeStruct((near, nodes...  9.36 us
    all_to_all x1, starting transfers between devices, local(): sent = lax.all_to_all(sent, 'cols', 0, 0, tiled=True)  4.66 us
    ppermute x1, starting transfers between devices, local(): far = lax.ppermute(far, 'cols', [(c, c ^ 2) for c in range(columns)])  3.46 us
    ppermute x1, starting transfers between devices, local(): near = lax.ppermute(given, 'cols', [(c, c ^ 1) for c in range(columns)])  3.09 us
    pallas_call x1, Pallas kernels, combine(): pl.pallas_call(combine_kernel, out_shape=jax.ShapeDtypeStruct((width, nod...  2.71 us
  transfers between devices with their start and end apart: 4, of which 3 were waited for; matrix products, arithmetic and copies ran while one was open for 0% of the time, Pallas kernels for 17%

profile of v6, /device:TPU:17, one launch (start us, length us, event | category | flops | bytes accessed | tf_op | source)
XLA Modules:
  0.0 73.4 jit_solution(9140848245395033700)
XLA Ops:
  0.0 2.3 %shard_map.82 = bf16[4,64,512]{2,1,0:T(8,128)(2,1)} custom-call(bf16[256,256]{1,0:T(8,128)(2,1)} %weight_hbm.1, bf16[192,256]{1,0:T(8,128)(2,1)} %refs_1_.1, bf16[192,512]{1,0:T(8,128)(2,1)} %refs_2_.1), custom_call_target="tpu_custom_call" | custom-call | flops 167772160 | bytes 1048576 | tf_op jit(solution)/shard_map/pallas_call | solution.py:60
  2.3 4.7 %all-to-all-start = ((bf16[4,64,512]{2,1,0:T(8,128)(2,1)}), bf16[4,64,512]{2,1,0:T(8,128)(2,1)S(1)}, u32[]{:S(2)}, u32[]{:S(2)}) async-start(bf16[4,64,512]{2,1,0:T(8,128)(2,1)} %shard_map.82), calls=%async_computation | async-start | bytes 524288 | tf_op jit(solution)/shard_map/all_to_all | solution.py:318
  6.9 1.8 %shard_map.83 = (f32[2,64,512]{2,1,0:T(8,128)S(1)}, bf16[2,64,512]{2,1,0:T(8,128)(2,1)S(1)}, s32[2,32,128]{2,1,0:T(8,128)S(1)}) custom-call(bf16[256,256]{1,0:T(8,128)(2,1)} %refs_0_.1, bf16[192,256]{1,0:T(8,128)(2,1)} %refs_1_.1, bf16[192,512]{1,0:T(8,128)(2,1)} %refs_2_.1, s32[1,8192]{1,0:T(1,128)} %refs_3_, s32[1,128]{1,0:T(1,128)} %refs_4_.1), custom_call_target="tpu_custom_call" | custom-call | flops 167772160 | bytes 1048576 | tf_op jit(solution)/shard_map/pallas_call | solution.py:112
  8.7 3.1 %collective-permute-start = (bf16[2,64,512]{2,1,0:T(8,128)(2,1)S(1)}, bf16[2,64,512]{2,1,0:T(8,128)(2,1)S(1)}, u32[]{:S(2)}, u32[]{:S(2)}) collective-permute-start(bf16[2,64,512]{2,1,0:T(8,128)(2,1)S(1)} %get-tuple-element.24), channel_id=1, source_target_pairs={{0,128},{128,0},{256,384},{384,256},{1,129},{129,1},{257,385},{385... | collective-permute-start | bytes 393224 | tf_op jit(solution)/shard_map/ppermute | solution.py:321
  11.8 0.0 all-to-all-done.sent
  11.8 1.7 %shard_map.84 = (bf16[4096,128]{1,0:T(8,128)(2,1)}, bf16[64,512]{1,0:T(8,128)(2,1)S(1)}) custom-call(bf16[4,64,512]{2,1,0:T(8,128)(2,1)S(1)} %all-to-all-done.sent, s32[2,32,128]{2,1,0:T(8,128)S(1)} %get-tuple-element.21.wanted), custom_call_target="tpu_custom_call" | custom-call | flops 536870912 | bytes 1048576 | tf_op jit(solution)/shard_map/pallas_call | solution.py:165
  13.5 2.3 %collective-permute-done.near = bf16[2,64,512]{2,1,0:T(8,128)(2,1)S(1)} collective-permute-done((bf16[2,64,512]{2,1,0:T(8,128)(2,1)S(1)}, bf16[2,64,512]{2,1,0:T(8,128)(2,1)S(1)}, u32[]{:S(2)}, u32[]{:S(2)}) %collective-permute-start) | collective-permute-done | bytes 131104 | tf_op jit(solution)/shard_map/ppermute | solution.py:321
  15.9 19.3 %all-to-all-start.1 = ((bf16[128,32,128]{2,1,0:T(8,128)(2,1)}), bf16[128,32,128]{2,1,0:T(8,128)(2,1)S(1)}, u32[]{:S(2)}, u32[]{:S(2)}) async-start(bf16[128,32,128]{2,1,0:T(8,128)(2,1)} %bitcast.8), calls=%async_computation.1 | async-start | bytes 2097152 | tf_op jit(solution)/shard_map/all_to_all | solution.py:327
  35.2 3.5 %collective-permute-start.1 = (bf16[64,512]{1,0:T(8,128)(2,1)S(1)}, bf16[64,512]{1,0:T(8,128)(2,1)S(1)}, u32[]{:S(2)}, u32[]{:S(2)}) collective-permute-start(bf16[64,512]{1,0:T(8,128)(2,1)S(1)} %fusion), channel_id=1, source_target_pairs={{0,256},{128,384},{256,0},{384,128},{1,257},{129,385},{257,1},{385... | collective-permute-start | bytes 196616 | tf_op jit(solution)/shard_map/ppermute | solution.py:328
  38.6 0.0 copy-start
  38.7 9.4 %shard_map.85 = (f8e4m3fn[3072,512]{1,0:T(32,128)(4,1)S(1)}, f8e4m3fn[5632,512]{1,0:T(32,128)(4,1)}) custom-call(s32[16,512]{1,0:T(8,128)} %neighbors_hbm, s32[1,512]{1,0:T(1,128)} %bitcast.6), custom_call_target="tpu_custom_call" | custom-call | flops 8999999488 | bytes 20971520 | tf_op jit(solution)/shard_map/pallas_call | solution.py:251
  48.0 11.4 %collective-permute-done.1.far = bf16[64,512]{1,0:T(8,128)(2,1)S(1)} collective-permute-done((bf16[64,512]{1,0:T(8,128)(2,1)S(1)}, bf16[64,512]{1,0:T(8,128)(2,1)S(1)}, u32[]{:S(2)}, u32[]{:S(2)}) %collective-permute-start.1) | collective-permute-done | bytes 65568 | tf_op jit(solution)/shard_map/ppermute | solution.py:328
  59.4 11.3 %all-to-all-done.1 = bf16[128,32,128]{2,1,0:T(8,128)(2,1)S(1)} async-done(((bf16[128,32,128]{2,1,0:T(8,128)(2,1)}), bf16[128,32,128]{2,1,0:T(8,128)(2,1)S(1)}, u32[]{:S(2)}, u32[]{:S(2)}) %all-to-all-start.1) | async-done | bytes 1048608 | tf_op jit(solution)/shard_map/all_to_all | solution.py:327
  70.7 0.0 copy-done
  70.7 2.7 %shard_map.86 = bf16[64,512]{1,0:T(8,128)(2,1)} custom-call(bf16[64,512]{1,0:T(8,128)(2,1)S(1)} %get-tuple-element.22.table, bf16[4096,128]{1,0:T(8,128)(2,1)S(1)} %bitcast.5, s32[1,512]{1,0:T(1,128)S(1)} %bitcast.7, f8e4m3fn[3072,512]{1,0:T(32,128)(4,1)S(1)} %get-tuple-element.30.first, f8e4m3fn[5632,512]{1,0:T(32,128)(4,1)} %get-tuple-element.31.counts_hbm, ...), custom_call_target="tpu_custom_call" | custom-call | flops 570425344 | bytes 10485760 | tf_op jit(solution)/shard_map/pallas_call | solution.py:302
  (1 shorter events, 0.0 us)
Async XLA Ops:
  2.3 9.6 %all-to-all-start = ((bf16[4,64,512]{2,1,0:T(8,128)(2,1)}), bf16[4,64,512]{2,1,0:T(8,128)(2,1)S(1)}, u32[]{:S(2)}, u32[]{:S(2)}) async-start(bf16[4,64,512]{2,1,0:T(8,128)(2,1)} %shard_map.82), calls=%async_computation | async-start | bytes 524288 | tf_op jit(solution)/shard_map/all_to_all | solution.py:318
  8.7 7.1 %collective-permute-start = (bf16[2,64,512]{2,1,0:T(8,128)(2,1)S(1)}, bf16[2,64,512]{2,1,0:T(8,128)(2,1)S(1)}, u32[]{:S(2)}, u32[]{:S(2)}) collective-permute-start(bf16[2,64,512]{2,1,0:T(8,128)(2,1)S(1)} %get-tuple-element.24), channel_id=1, source_target_pairs={{0,128},{128,0},{256,384},{384,256},{1,129},{129,1},{257,385},{385... | collective-permute-start | bytes 393224 | tf_op jit(solution)/shard_map/ppermute | solution.py:321
  15.9 54.8 %all-to-all-start.1 = ((bf16[128,32,128]{2,1,0:T(8,128)(2,1)}), bf16[128,32,128]{2,1,0:T(8,128)(2,1)S(1)}, u32[]{:S(2)}, u32[]{:S(2)}) async-start(bf16[128,32,128]{2,1,0:T(8,128)(2,1)} %bitcast.8), calls=%async_computation.1 | async-start | bytes 2097152 | tf_op jit(solution)/shard_map/all_to_all | solution.py:327
  35.2 24.2 %collective-permute-start.1 = (bf16[64,512]{1,0:T(8,128)(2,1)S(1)}, bf16[64,512]{1,0:T(8,128)(2,1)S(1)}, u32[]{:S(2)}, u32[]{:S(2)}) collective-permute-start(bf16[64,512]{1,0:T(8,128)(2,1)S(1)} %fusion), channel_id=1, source_target_pairs={{0,256},{128,384},{256,0},{384,128},{1,257},{129,385},{257,1},{385... | collective-permute-start | bytes 196616 | tf_op jit(solution)/shard_map/ppermute | solution.py:328
  38.6 32.0 %copy-start = (s32[512]{0:T(512)S(1)}, s32[512]{0:T(512)}, u32[]{:S(2)}) copy-start(s32[512]{0:T(512)} %param.13) | copy-start | bytes 6148

commit v7 on v6

--- a/solution.py
+++ b/solution.py
@@ -246,7 +246,7 @@
 
 def count(neighbors, degree, rows):
     slots, nodes = neighbors.shape
-    near = PACK * 128 * 4
+    near = PACK * 128 * 5
     arrays = (neighbors, degree)
     return pl.pallas_call(
         count_kernel,
@@ -269,27 +269,31 @@
     width, nodes = table.shape
     depth = rows.shape[0]
     chunk = 512
-    copies = []
-    for i in range(second.shape[0] // chunk):
-        at = pl.ds(i * chunk, chunk)
-        copies.append(pltpu.make_async_copy(counts_hbm.at[at], second.at[at], arrived.at[i]))
-        copies[i].start()
+    pieces = []
+    for start in range(0, nodes + 2 * depth, chunk):
+        middle = min(max(first.shape[0], start), start + chunk)
+        pieces += [(low, high - low) for low, high in ((start, middle), (middle, start + chunk)) if high > low]
+    copies = {}
+    for start, size in pieces:
+        if start >= first.shape[0]:
+            at = pl.ds(start - first.shape[0], size)
+            copies[start] = pltpu.make_async_copy(counts_hbm.at[at], second.at[at], arrived.at[len(copies)])
+            copies[start].start()
     turned = []
     total = jnp.zeros((width, nodes), F32)
-    for start in range(0, nodes + 2 * depth, chunk):
+    for start, size in pieces:
         if start < nodes:
-            left = table[:, start : start + chunk]
+            left = table[:, start : start + size]
         else:
             h, low = divmod(start - nodes, depth)
-            if h == 0:
+            if h == 0 and low % chunk == 0:
                 turned.append(rows[low : low + chunk, :].astype(F32).T.astype(BF16))
-            left = turned[low // chunk][h * width : (h + 1) * width]
+            left = turned[low // chunk][h * width : (h + 1) * width, low % chunk : low % chunk + size]
         if start < first.shape[0]:
-            counts = first[pl.ds(start, chunk), :]
+            counts = first[pl.ds(start, size), :]
         else:
-            at = start - first.shape[0]
-            copies[at // chunk].wait()
-            counts = second[pl.ds(at, chunk), :]
+            copies[start].wait()
+            counts = second[pl.ds(start - first.shape[0], size), :]
         total = total + dot(left, counts, ((1,), (0,)))
     own = kept[0] + near[0].astype(F32) + far[...].astype(F32)
     result = own + total / degree[...].astype(F32)
@@ -304,7 +308,7 @@
         out_shape=jax.ShapeDtypeStruct((width, nodes), BF16),
         in_specs=[VMEM] * 4 + [ANY] + [VMEM] * 3,
         out_specs=VMEM,
-        scratch_shapes=[pltpu.VMEM(second.shape, F8), pltpu.SemaphoreType.DMA((second.shape[0] // 512,))],
+        scratch_shapes=[pltpu.VMEM(second.shape, F8), pltpu.SemaphoreType.DMA((pl.cdiv(second.shape[0], 512),))],
         compiler_params=LIMIT,
         cost_estimate=cost(2 * width * nodes * 8704, 10 << 20),
     )(table, rows, degree, first, *in_hbm([second]), kept, near, far)

time: 73.8 us -> 74.4 us (level)
  no operation moved by 1% of the time
where the time goes in v7:
time: 74.4 us; the launch traced here: 74 us
  starting transfers between devices  30.5 us (41%)
  waiting for transfers between devices  25.1 us (34%)
  Pallas kernels  17.7 us (24%)
    all_to_all x1, starting transfers between devices, local(): lax.all_to_all(chosen.reshape(-1, HALF, chosen.shape[1]), 'dom', 0, 0, ti...  19.3 us
    all_to_all x1, waiting for transfers between devices, local(): lax.all_to_all(chosen.reshape(-1, HALF, chosen.shape[1]), 'dom', 0, 0, ti...  11.4 us
    ppermute x1, waiting for transfers between devices, local(): far = lax.ppermute(far, 'cols', [(c, c ^ 2) for c in range(columns)])  11.3 us
    pallas_call x1, Pallas kernels, count(): pl.pallas_call(count_kernel, out_shape=(jax.ShapeDtypeStruct((near, nodes...  9.31 us
    all_to_all x1, starting transfers between devices, local(): sent = lax.all_to_all(sent, 'cols', 0, 0, tiled=True)  4.66 us
    ppermute x1, starting transfers between devices, local(): far = lax.ppermute(far, 'cols', [(c, c ^ 2) for c in range(columns)])  3.45 us
    ppermute x1, starting transfers between devices, local(): near = lax.ppermute(given, 'cols', [(c, c ^ 1) for c in range(columns)])  3.09 us
    pallas_call x1, Pallas kernels, combine(): pl.pallas_call(combine_kernel, out_shape=jax.ShapeDtypeStruct((width, nod...  2.65 us
  transfers between devices with their start and end apart: 4, of which 3 were waited for; matrix products, arithmetic and copies ran while one was open for 0% of the time, Pallas kernels for 17%

profile of v7, /device:TPU:17, one launch (start us, length us, event | category | flops | bytes accessed | tf_op | source)
XLA Modules:
  0.0 74.0 jit_solution(7282952052402941171)
XLA Ops:
  0.0 2.3 %shard_map.82 = bf16[4,64,512]{2,1,0:T(8,128)(2,1)} custom-call(bf16[256,256]{1,0:T(8,128)(2,1)} %weight_hbm.1, bf16[192,256]{1,0:T(8,128)(2,1)} %refs_1_.1, bf16[192,512]{1,0:T(8,128)(2,1)} %refs_2_.1), custom_call_target="tpu_custom_call" | custom-call | flops 167772160 | bytes 1048576 | tf_op jit(solution)/shard_map/pallas_call | solution.py:60
  2.3 4.7 %all-to-all-start = ((bf16[4,64,512]{2,1,0:T(8,128)(2,1)}), bf16[4,64,512]{2,1,0:T(8,128)(2,1)S(1)}, u32[]{:S(2)}, u32[]{:S(2)}) async-start(bf16[4,64,512]{2,1,0:T(8,128)(2,1)} %shard_map.82), calls=%async_computation | async-start | bytes 524288 | tf_op jit(solution)/shard_map/all_to_all | solution.py:322
  6.9 1.8 %shard_map.83 = (f32[2,64,512]{2,1,0:T(8,128)S(1)}, bf16[2,64,512]{2,1,0:T(8,128)(2,1)S(1)}, s32[2,32,128]{2,1,0:T(8,128)S(1)}) custom-call(bf16[256,256]{1,0:T(8,128)(2,1)} %refs_0_.1, bf16[192,256]{1,0:T(8,128)(2,1)} %refs_1_.1, bf16[192,512]{1,0:T(8,128)(2,1)} %refs_2_.1, s32[1,8192]{1,0:T(1,128)} %refs_3_, s32[1,128]{1,0:T(1,128)} %refs_4_.1), custom_call_target="tpu_custom_call" | custom-call | flops 167772160 | bytes 1048576 | tf_op jit(solution)/shard_map/pallas_call | solution.py:112
  8.7 3.1 %collective-permute-start = (bf16[2,64,512]{2,1,0:T(8,128)(2,1)S(1)}, bf16[2,64,512]{2,1,0:T(8,128)(2,1)S(1)}, u32[]{:S(2)}, u32[]{:S(2)}) collective-permute-start(bf16[2,64,512]{2,1,0:T(8,128)(2,1)S(1)} %get-tuple-element.24), channel_id=1, source_target_pairs={{0,128},{128,0},{256,384},{384,256},{1,129},{129,1},{257,385},{385... | collective-permute-start | bytes 393224 | tf_op jit(solution)/shard_map/ppermute | solution.py:325
  11.8 0.0 all-to-all-done.sent
  11.8 1.7 %shard_map.84 = (bf16[4096,128]{1,0:T(8,128)(2,1)}, bf16[64,512]{1,0:T(8,128)(2,1)S(1)}) custom-call(bf16[4,64,512]{2,1,0:T(8,128)(2,1)S(1)} %all-to-all-done.sent, s32[2,32,128]{2,1,0:T(8,128)S(1)} %get-tuple-element.21.wanted), custom_call_target="tpu_custom_call" | custom-call | flops 536870912 | bytes 1048576 | tf_op jit(solution)/shard_map/pallas_call | solution.py:165
  13.5 2.3 %collective-permute-done.near = bf16[2,64,512]{2,1,0:T(8,128)(2,1)S(1)} collective-permute-done((bf16[2,64,512]{2,1,0:T(8,128)(2,1)S(1)}, bf16[2,64,512]{2,1,0:T(8,128)(2,1)S(1)}, u32[]{:S(2)}, u32[]{:S(2)}) %collective-permute-start) | collective-permute-done | bytes 131104 | tf_op jit(solution)/shard_map/ppermute | solution.py:325
  15.9 0.6 fusion
  16.5 19.3 %all-to-all-start.1 = ((bf16[128,32,128]{2,1,0:T(8,128)(2,1)}), bf16[128,32,128]{2,1,0:T(8,128)(2,1)S(1)}, u32[]{:S(2)}, u32[]{:S(2)}) async-start(bf16[128,32,128]{2,1,0:T(8,128)(2,1)} %bitcast.8), calls=%async_computation.1 | async-start | bytes 2097152 | tf_op jit(solution)/shard_map/all_to_all | solution.py:331
  35.8 3.4 %collective-permute-start.1 = (bf16[64,512]{1,0:T(8,128)(2,1)}, bf16[64,512]{1,0:T(8,128)(2,1)S(1)}, u32[]{:S(2)}, u32[]{:S(2)}) collective-permute-start(bf16[64,512]{1,0:T(8,128)(2,1)} %fusion), channel_id=1, source_target_pairs={{0,256},{128,384},{256,0},{384,128},{1,257},{129,385},{257,1},{385... | collective-permute-start | bytes 196616 | tf_op jit(solution)/shard_map/ppermute | solution.py:332
  39.2 0.0 copy-start
  39.3 9.3 %shard_map.85 = (f8e4m3fn[3840,512]{1,0:T(32,128)(4,1)S(1)}, f8e4m3fn[4864,512]{1,0:T(32,128)(4,1)}) custom-call(s32[16,512]{1,0:T(8,128)} %neighbors_hbm, s32[1,512]{1,0:T(1,128)} %bitcast.6), custom_call_target="tpu_custom_call" | custom-call | flops 8999999488 | bytes 20971520 | tf_op jit(solution)/shard_map/pallas_call | solution.py:251
  48.6 11.3 %collective-permute-done.1.far = bf16[64,512]{1,0:T(8,128)(2,1)S(1)} collective-permute-done((bf16[64,512]{1,0:T(8,128)(2,1)}, bf16[64,512]{1,0:T(8,128)(2,1)S(1)}, u32[]{:S(2)}, u32[]{:S(2)}) %collective-permute-start.1) | collective-permute-done | bytes 65568 | tf_op jit(solution)/shard_map/ppermute | solution.py:332
  59.9 11.4 %all-to-all-done.1 = bf16[128,32,128]{2,1,0:T(8,128)(2,1)S(1)} async-done(((bf16[128,32,128]{2,1,0:T(8,128)(2,1)}), bf16[128,32,128]{2,1,0:T(8,128)(2,1)S(1)}, u32[]{:S(2)}, u32[]{:S(2)}) %all-to-all-start.1) | async-done | bytes 1048608 | tf_op jit(solution)/shard_map/all_to_all | solution.py:331
  71.3 0.0 copy-done
  71.3 2.7 %shard_map.86 = bf16[64,512]{1,0:T(8,128)(2,1)} custom-call(bf16[64,512]{1,0:T(8,128)(2,1)S(1)} %get-tuple-element.22.table, bf16[4096,128]{1,0:T(8,128)(2,1)S(1)} %bitcast.5, s32[1,512]{1,0:T(1,128)S(1)} %bitcast.7, f8e4m3fn[3840,512]{1,0:T(32,128)(4,1)S(1)} %get-tuple-element.30.first, f8e4m3fn[4864,512]{1,0:T(32,128)(4,1)} %get-tuple-element.31.counts_hbm, ...), custom_call_target="tpu_custom_call" | custom-call | flops 570425344 | bytes 10485760 | tf_op jit(solution)/shard_map/pallas_call | solution.py:306
Async XLA Ops:
  2.3 9.6 %all-to-all-start = ((bf16[4,64,512]{2,1,0:T(8,128)(2,1)}), bf16[4,64,512]{2,1,0:T(8,128)(2,1)S(1)}, u32[]{:S(2)}, u32[]{:S(2)}) async-start(bf16[4,64,512]{2,1,0:T(8,128)(2,1)} %shard_map.82), calls=%async_computation | async-start | bytes 524288 | tf_op jit(solution)/shard_map/all_to_all | solution.py:322
  8.7 7.1 %collective-permute-start = (bf16[2,64,512]{2,1,0:T(8,128)(2,1)S(1)}, bf16[2,64,512]{2,1,0:T(8,128)(2,1)S(1)}, u32[]{:S(2)}, u32[]{:S(2)}) collective-permute-start(bf16[2,64,512]{2,1,0:T(8,128)(2,1)S(1)} %get-tuple-element.24), channel_id=1, source_target_pairs={{0,128},{128,0},{256,384},{384,256},{1,129},{129,1},{257,385},{385... | collective-permute-start | bytes 393224 | tf_op jit(solution)/shard_map/ppermute | solution.py:325
  16.5 54.8 %all-to-all-start.1 = ((bf16[128,32,128]{2,1,0:T(8,128)(2,1)}), bf16[128,32,128]{2,1,0:T(8,128)(2,1)S(1)}, u32[]{:S(2)}, u32[]{:S(2)}) async-start(bf16[128,32,128]{2,1,0:T(8,128)(2,1)} %bitcast.8), calls=%async_computation.1 | async-start | bytes 2097152 | tf_op jit(solution)/shard_map/all_to_all | solution.py:331
  35.8 24.1 %collective-permute-start.1 = (bf16[64,512]{1,0:T(8,128)(2,1)}, bf16[64,512]{1,0:T(8,128)(2,1)S(1)}, u32[]{:S(2)}, u32[]{:S(2)}) collective-permute-start(bf16[64,512]{1,0:T(8,128)(2,1)} %fusion), channel_id=1, source_target_pairs={{0,256},{128,384},{256,0},{384,128},{1,257},{129,385},{257,1},{385... | collective-permute-start | bytes 196616 | tf_op jit(solution)/shard_map/ppermute | solution.py:332
  39.2 32.1 %copy-start = (s32[512]{0:T(512)S(1)}, s32[512]{0:T(512)}, u32[]{:S(2)}) copy-start(s32[512]{0:T(512)} %param.13) | copy-start | bytes 6148
